TPU v7x, 128 devices: a whole 4x4x4 slice. The times are simulated.
128 devices in a mesh: pipe: 8 (over x, y_lo), tensor: 4 (over z), dp: 4 (over y_hi, core).
Axes of the slice: x: 4, y: 4 (y_hi: 2, y_lo: 2; y = y_hi * 2 + y_lo), z: 4, core: 2. Of those that a mesh axis runs over, the one named last changes fastest.
Arguments:
- new_coeffs: bfloat16 [1024, 256], P('dp'), may hold values from -6 to 6
- loss_grad: bfloat16 [1024, 256], P('dp'), may hold values from -6 to 6
- sent_forward: bfloat16 [8, 1024, 256], P('pipe', 'dp'), may hold values from -6 to 6
- sent_backward: bfloat16 [8, 1024, 256], P('pipe', 'dp'), may hold values from -6 to 6
- stashed: bfloat16 [8, 1024, 256], P('pipe', 'dp'), may hold values from -6 to 6
- subspace: bfloat16 [4096, 256], replicated, may hold values from -0.09375 to 0.09375
- norm_gain: float32 [8, 4096], P('pipe'), may hold values from 0.5 to 1.5
- w_query: bfloat16 [8, 4096, 4096], P('pipe', None, 'tensor'), may hold values from -3 to 3
- w_key: bfloat16 [8, 4096, 512], P('pipe', None, 'tensor'), may hold values from -3 to 3
- w_value: bfloat16 [8, 4096, 512], P('pipe', None, 'tensor'), may hold values from -0.09375 to 0.09375
- w_output: bfloat16 [8, 4096, 4096], P('pipe', 'tensor'), may hold values from -0.09375 to 0.09375
Outputs:
- forward_out: bfloat16 [8, 1024, 256], P('pipe', 'dp')
- backward_out: bfloat16 [8, 1024, 256], P('pipe', 'dp')
- grad_query: bfloat16 [8, 4096, 4096], P('pipe', 'dp', 'tensor')
- grad_key: bfloat16 [8, 4096, 512], P('pipe', 'dp', 'tensor')
- grad_value: bfloat16 [8, 4096, 512], P('pipe', 'dp', 'tensor')
- grad_output: bfloat16 [8, 4096, 4096], P('pipe', 'tensor', 'dp')
- grad_gain: float32 [8, 4096], P('pipe')
All inputs are finite; a program needn't handle non-finite values.
Results may differ from a plain program's by a relative error of at most 0.015.
Values may be sent and summed in bfloat16 or wider, within the bound.
A program may use at most 192 MiB of HBM per device.

v0:
```python
import math

import jax
import jax.numpy as jnp
from jax import lax
from jax.sharding import PartitionSpec as P

HD = 128
EPSILON = 1e-05
ROPE_BASE = 500000.0
BF16 = jnp.bfloat16
F32 = jnp.float32


def shifted(x, axis, by):
    devices = lax.axis_size(axis)
    pairs = [(i, i + by) for i in range(devices) if 0 <= i + by < devices]
    return lax.ppermute(x, axis, pairs)


def rope_tables(length, head_width):
    half_width = head_width // 2
    frequency = ROPE_BASE ** (-2.0 * jnp.arange(half_width, dtype=F32) / head_width)
    angles = jnp.arange(length, dtype=F32)[:, None] * frequency[None, :]
    angles = jnp.concatenate([angles, angles], axis=1)
    return (jnp.cos(angles), jnp.sin(angles))


def rotate_half(values):
    half_width = values.shape[-1] // 2
    return jnp.concatenate([-values[..., half_width:], values[..., :half_width]], axis=-1)


def apply_rope(values, cosine, sine_table):
    return values * cosine[:, None, :] + rotate_half(values) * sine_table[:, None, :]


def undo_rope(values, cosine, sine_table):
    return values * cosine[:, None, :] - rotate_half(values) * sine_table[:, None, :]


def dot(spec, a, b):
    return jnp.einsum(spec, a, b, preferred_element_type=F32)


def heads(coeffs, gram, width, query_c, key_c, value_c, cosine, sine_table):
    length = coeffs.shape[0]
    wide = coeffs.astype(F32)
    projected = jnp.dot(wide, gram, precision=lax.Precision.HIGHEST)
    square = jnp.maximum(jnp.sum(projected * wide, axis=-1, keepdims=True), 0.0) / width
    inverse = 1.0 / jnp.sqrt(square + EPSILON)
    query_rows = (dot("tr,re->te", coeffs, query_c) * inverse).reshape(length, -1, HD)
    query_rows = apply_rope(query_rows, cosine, sine_table).astype(BF16)
    key_rows = (dot("tr,re->te", coeffs, key_c) * inverse).reshape(length, -1, HD)
    key_rows = apply_rope(key_rows, cosine, sine_table).astype(BF16)
    value_rows = (dot("tr,re->te", coeffs, value_c) * inverse).astype(BF16).reshape(length, -1, HD)
    key_heads = key_rows.shape[1]
    grouped = query_rows.reshape(length, key_heads, -1, HD)
    scores = dot("tkgd,ukd->kgtu", grouped, key_rows) / math.sqrt(HD)
    causal = jnp.arange(length)[:, None] >= jnp.arange(length)[None, :]
    scores = jnp.where(causal, scores, -jnp.inf)
    row_max = jnp.max(scores, axis=-1, keepdims=True)
    exps = jnp.exp(scores - row_max)
    probs_full = exps / jnp.sum(exps, axis=-1, keepdims=True)
    probs_low = probs_full.astype(BF16)
    head_out = dot("kgtu,ukd->tkgd", probs_low, value_rows).astype(BF16).reshape(length, -1)
    return projected, inverse, grouped, key_rows, value_rows, probs_full, probs_low, head_out


def body(
    new_coeffs,
    loss_grad,
    sent_forward,
    sent_backward,
    stashed,
    subspace,
    norm_gain,
    w_query,
    w_key,
    w_value,
    w_output,
):
    section_index = lax.axis_index("pipe")
    last_section = lax.axis_size("pipe") - 1
    arrived = shifted(sent_forward[0], "pipe", 1)
    returned = shifted(sent_backward[0], "pipe", -1)
    inputs = jnp.where(section_index == 0, new_coeffs, arrived)
    upstream = jnp.where(section_index == last_section, loss_grad, returned)
    saved = stashed[0]
    length = inputs.shape[0]
    width = subspace.shape[0]
    cosine, sine_table = rope_tables(length, HD)
    gain_row = norm_gain[0]
    query_w = w_query[0]
    key_w = w_key[0]
    value_w = w_value[0]
    output_w = w_output[0]
    basis_scaled = (subspace * gain_row[:, None]).astype(BF16)
    gram = dot("dr,ds->rs", subspace, subspace)
    query_c = dot("dr,de->re", basis_scaled, query_w).astype(BF16)
    key_c = dot("dr,de->re", basis_scaled, key_w).astype(BF16)
    value_c = dot("dr,de->re", basis_scaled, value_w).astype(BF16)
    output_c = dot("ed,dr->er", output_w, subspace).astype(BF16)
    tables = (gram, width, query_c, key_c, value_c, cosine, sine_table)
    projected, _, _, _, _, _, _, head_out = heads(inputs, *tables)
    forward_part = dot("te,er->tr", head_out, output_c)
    projected_b, inverse, grouped, key_rows, value_rows, probs_full, probs_low, head_out = heads(
        saved, *tables
    )
    key_heads = key_rows.shape[1]
    group_size = grouped.shape[2]
    output_term = dot("te,tr->er", head_out, upstream)
    grad_heads = dot("tr,er->te", upstream, output_c)
    grad_heads = grad_heads.astype(BF16).reshape(length, key_heads, group_size, HD)
    grad_values = dot("kgtu,tkgd->ukd", probs_low, grad_heads)
    grad_probs = dot("tkgd,ukd->kgtu", grad_heads, value_rows)
    centred = grad_probs - jnp.sum(probs_full * grad_probs, axis=-1, keepdims=True)
    scores_low = (probs_full * centred / math.sqrt(HD)).astype(BF16)
    grad_query = dot("kgtu,ukd->tkgd", scores_low, key_rows).reshape(length, -1, HD)
    grad_keys = dot("kgtu,tkgd->ukd", scores_low, grouped)
    grad_query = undo_rope(grad_query, cosine, sine_table).astype(BF16).reshape(length, -1)
    grad_keys = undo_rope(grad_keys, cosine, sine_table).astype(BF16).reshape(length, -1)
    grad_values = grad_values.astype(BF16).reshape(length, -1)
    scaled_coeffs = (saved * inverse).astype(BF16)
    query_term = dot("tr,te->re", scaled_coeffs, grad_query)
    key_term = dot("tr,te->re", scaled_coeffs, grad_keys)
    value_term = dot("tr,te->re", scaled_coeffs, grad_values)
    backward_part = dot("te,re->tr", grad_query, query_c)
    backward_part = backward_part + dot("te,re->tr", grad_keys, key_c)
    backward_part = backward_part + dot("te,re->tr", grad_values, value_c)
    forward_sum, backward_sum = lax.psum(
        (forward_part.astype(BF16), backward_part.astype(BF16)), "tensor"
    )
    forward_coeffs = (projected + forward_sum.astype(F32)).astype(BF16)
    backward_sum = backward_sum.astype(F32)
    middle = jnp.sum(backward_sum * saved, axis=-1, keepdims=True) * (inverse / width)
    grad_coeffs = (backward_sum - projected_b * (inverse * middle)) * inverse
    lifted = jnp.dot(upstream.astype(F32), gram, precision=lax.Precision.HIGHEST)
    backward_coeffs = (lifted + grad_coeffs).astype(BF16)
    query_term, key_term, value_term, output_term = lax.psum(
        (
            query_term.astype(BF16),
            key_term.astype(BF16),
            value_term.astype(BF16),
            output_term.astype(BF16),
        ),
        "dp",
    )
    part = lax.axis_index("dp")
    rows = width // lax.axis_size("dp")
    own_basis = lax.dynamic_slice_in_dim(subspace, part * rows, rows, 0)
    own_gain = lax.dynamic_slice_in_dim(gain_row, part * rows, rows, 0)[:, None]
    own_query, own_key, own_value = [
        lax.dynamic_slice_in_dim(w, part * rows, rows, 0) for w in (query_w, key_w, value_w)
    ]
    query_sum = dot("dr,re->de", own_basis, query_term)
    key_sum = dot("dr,re->de", own_basis, key_term)
    value_sum = dot("dr,re->de", own_basis, value_term)
    output_sum = dot("er,dr->ed", output_term, own_basis)
    gain_part = (
        jnp.sum(query_sum * own_query, axis=1)
        + jnp.sum(key_sum * own_key, axis=1)
        + jnp.sum(value_sum * own_value, axis=1)
    )
    grad_gain = lax.all_gather(lax.psum(gain_part, "tensor"), "dp", tiled=True)
    return (
        forward_coeffs[None],
        backward_coeffs[None],
        (query_sum * own_gain).astype(BF16)[None],
        (key_sum * own_gain).astype(BF16)[None],
        (value_sum * own_gain).astype(BF16)[None],
        output_sum.astype(BF16)[None],
        grad_gain[None],
    )


def solution(mesh):
    return jax.shard_map(
        body,
        mesh=mesh,
        in_specs=(
            P("dp", None),
            P("dp", None),
            P("pipe", "dp", None),
            P("pipe", "dp", None),
            P("pipe", "dp", None),
            P(),
            P("pipe", None),
            P("pipe", None, "tensor"),
            P("pipe", None, "tensor"),
            P("pipe", None, "tensor"),
            P("pipe", "tensor", None),
        ),
        out_specs=(
            P("pipe", "dp", None),
            P("pipe", "dp", None),
            P("pipe", "dp", "tensor"),
            P("pipe", "dp", "tensor"),
            P("pipe", "dp", "tensor"),
            P("pipe", "tensor", "dp"),
            P("pipe", None),
        ),
        check_vma=False,
    )
```

profile of v0, /device:TPU:1, one launch (start us, length us, event | category | flops | bytes accessed | tf_op | source)
XLA Modules:
  0.0 238.1 jit_solution(7652917388349691554)
XLA Ops:
  7.2 1.7 copy.52
  8.9 4.7 %collective-permute-start = (bf16[256,256]{0,1:T(8,128)(2,1)}, bf16[256,256]{0,1:T(8,128)(2,1)}, u32[]{:S(2)}, u32[]{:S(2)}) collective-permute-start(bf16[256,256]{0,1:T(8,128)(2,1)} %bitcast), channel_id=1, source_target_pairs={{0,16},{16,32},{32,48},{48,64},{64,80},{80,96},{96,112},{1,17},{17... | collective-permute-start | bytes 393224 | tf_op jit(solution)/shard_map/ppermute | solution.py:18
  13.6 1.3 collective-permute-start.1
  14.9 3.1 %fusion.106 = f32[256,256]{1,0:T(8,128)S(1)} fusion(bf16[4096,256]{1,0:T(8,128)(2,1)} %param.16), kind=kOutput, calls=%fused_computation.170 | convolution fusion | flops 536870912 | bytes 2359296 | tf_op jit(solution)/shard_map/dr,ds->rs/dot_general | solution.py:43
  18.0 1.0 fusion.55
  19.7 6.0 %fusion.14 = bf16[256,1024]{1,0:T(8,128)(2,1)S(1)} fusion(bf16[1,4096,1024]{2,1,0:T(8,128)(2,1)} %param.18, bf16[4096,256]{1,0:T(8,128)(2,1)S(1)} %copy-done, f32[4096]{0:T(1024)S(1)} %bitcast.264), kind=kOutput, calls=%fused_computation.27 | convolution fusion | flops 2150891520 | bytes 11026432 | tf_op jit(solution)/shard_map/dr,de->re/dot_general | solution.py:43
  25.7 1.4 convolution_convert_fusion.6
  27.1 1.3 fusion.13
  29.3 2.0 convolution_convert_fusion.7
  31.4 3.1 %fusion.17 = bf16[1024,256]{1,0:T(8,128)(2,1)} fusion(bf16[4096,256]{1,0:T(8,128)(2,1)S(1)} %copy-done, bf16[1,1024,4096]{2,1,0:T(8,128)(2,1)S(1)} %bitcast.272), kind=kOutput, calls=%fused_computation.28 | convolution fusion | flops 2147745792 | bytes 11010048 | tf_op jit(solution)/shard_map/ed,dr->er/dot_general | solution.py:43
  34.5 1.2 fusion.78
  37.1 1.6 copy.108
  38.7 2.1 mul.337
  40.8 2.5 %copy.99 = f32[256,1024]{1,0:T(8,128)} copy(f32[256,1024]{0,1:T(8,128)} %bitcast.254) | data formatting | bytes 2097152 | tf_op jit(solution)/shard_map/mul | solution.py:35
  43.3 1.7 fusion.27
  45.0 0.9 broadcast_select_fusion.1
  46.0 1.1 multiply_reduce_fusion
  47.1 2.3 convolution_multiply_fusion.1
  49.5 0.9 convolution_multiply_fusion.4
  50.3 2.5 %copy.107 = f32[256,1024]{0,1:T(8,128)} copy(f32[256,1024]{1,0:T(8,128)} %convolution_multiply_fusion.1) | data formatting | bytes 2097152 | tf_op jit(solution)/shard_map/reshape | solution.py:52
  52.9 1.4 slice_negate_fusion.1
  54.3 1.6 maximum_multiply_fusion.1
  55.9 2.7 %copy.102 = f32[256,1024]{1,0:T(8,128)} copy(f32[256,1024]{0,1:T(8,128)} %bitcast.252) | data formatting | bytes 2097152 | tf_op jit(solution)/shard_map/mul | solution.py:35
  58.6 2.6 %copy.100 = f32[256,1024]{1,0:T(8,128)} copy(f32[256,1024]{0,1:T(8,128)} %bitcast.255) | data formatting | bytes 2097152 | tf_op jit(solution)/shard_map/mul | solution.py:35
  61.1 3.6 %fusion.36 = (bf16[32,8,8,128]{3,2,1,0:T(8,128)(2,1)S(1)}, bf16[32,8,8,128]{3,2,1,0:T(8,128)(2,1)}) fusion(f32[256,1024]{1,0:T(8,128)} %copy.102, f32[256,1024]{1,0:T(8,128)S(1)} %copy-done.3, f32[256,1024]{1,0:T(8,128)} %copy.99, f32[256,1024]{1,0:T(8,128)} %copy.100, f32[256,1024]{1,0:T(8,128)} %convolution_multiply_fusion.1), kind=kLoop, calls=%fused_computation.75 | loop fusion | flops 1572864 | bytes 6291456
  65.8 0.9 broadcast_select_fusion
  68.5 1.6 convert_bitcast_fusion.1
  70.5 0.9 copy-done.2
  71.7 1.1 convolution_bitcast_fusion.2
  72.9 2.7 %copy.96 = bf16[8,256,256]{2,0,1:T(8,128)(2,1)} copy(bf16[8,256,256]{1,2,0:T(8,128)(2,1)} %get-tuple-element.29) | data formatting | bytes 2097152 | tf_op jit(solution)/shard_map/reshape.46
  75.5 2.4 %convolution_convert_fusion.1 = bf16[128,8,256]{2,0,1:T(8,128)(2,1)} fusion(bf16[128,256,1]{1,0,2:T(8,128)(2,1)} %fusion.27, bf16[8,256,256]{1,2,0:T(8,128)(2,1)} %get-tuple-element.29), kind=kOutput, calls=%fused_computation.30 | convolution fusion | flops 134479872 | bytes 1638400 | tf_op jit(solution)/shard_map/kgtu,ukd->tkgd/dot_general | solution.py:43
  77.9 0.9 fusion.82
  78.8 2.1 fusion.98
  80.9 1.3 copy-done.6
  82.2 0.9 fusion.10
  83.1 3.1 %convolution_convert_fusion.4 = bf16[128,8,256]{2,0,1:T(8,128)(2,1)} fusion(f32[1,8,256,256]{2,3,1,0:T(8,128)} %copy-done.6, f32[8,256]{1,0:T(8,128)} %fusion.10, f32[8,256]{1,0:T(8,128)} %copy-done.44, bf16[256,256]{0,1:T(8,128)(2,1)} %copy-done.15, bf16[256,128]{1,0:T(8,128)(2,1)} %convolution_convert_fusion.7, f32[256]{0:T(256)} %copy-done.45), kind=kOutput, calls=%fused_computation.33 | convolution fusion | flops 152895488 | bytes 2835456 | tf_op jit(solution)/shard_map/kgtu,ukd->tkgd/dot_general | solution.py:43
  86.2 2.2 convolution_convert_fusion.5
  88.5 1.2 fusion.97
  89.7 1.1 maximum_multiply_fusion.2
  90.8 2.5 %copy.105 = f32[256,1024]{1,0:T(8,128)} copy(f32[256,1024]{0,1:T(8,128)} %bitcast.253) | data formatting | bytes 2097152 | tf_op jit(solution)/shard_map/mul | solution.py:39
  93.3 1.3 copy.104
  94.6 0.9 slice_negate_fusion.3
  95.5 1.4 fusion.72
  96.9 1.6 convolution_convert_fusion.9
  98.5 2.5 %fusion.37 = f32[256,256]{1,0:T(8,128)S(1)} fusion(bf16[256,1024]{1,0:T(8,128)(2,1)} %copy-done.5, f32[256,1024]{1,0:T(8,128)} %copy.105, f32[256,1024]{1,0:T(8,128)} %copy.104, f32[256,1024]{1,0:T(8,128)} %copy.99), kind=kOutput, calls=%fused_computation.76 | convolution fusion | flops 135004160 | bytes 3932160 | tf_op jit(solution)/shard_map/te,re->tr/dot_general | solution.py:43
  101.4 1.1 convolution_convert_fusion
  103.5 0.9 fusion.21
  104.7 1.5 fusion.31
  106.2 0.9 convolution_convert_fusion.8
  107.1 1.2 convolution_convert_fusion.2
  108.4 3.1 %constant_dynamic-slice_fusion.2 = bf16[1,1024,1024]{2,1,0:T(8,128)(2,1)} fusion(bf16[1,4096,1024]{2,1,0:T(8,128)(2,1)} %param.18, s32[]{:T(128)S(6)} %select_n.34), kind=kLoop, calls=%fused_computation.158 | loop fusion | bytes 4194308 | tf_op jit(solution)/shard_map/dynamic_slice | solution.py:154
  111.5 3.9 %copy.109 = bf16[1,1024,1024]{1,2,0:T(8,128)(2,1)} copy(bf16[1,1024,1024]{2,1,0:T(8,128)(2,1)} %constant_dynamic-slice_fusion.2) | data formatting | bytes 4194304
  115.4 1.8 constant_dynamic-slice_fusion
  118.1 1.1 copy.111
  119.8 28.7 %all-reduce.7.cloned.1.call-done = (bf16[256,256]{0,1:T(8,128)(2,1)}, bf16[256,256]{1,0:T(8,128)(2,1)}) async-done(((bf16[256,256]{0,1:T(8,128)(2,1)}, bf16[256,256]{1,0:T(8,128)(2,1)}), (bf16[256,256]{0,1:T(8,128)(2,1)}, bf16[256,256]{1,0:T(8,128)(2,1)})) %all-reduce.7.cloned.1.call-update) | async-done | bytes 262160 | tf_op jit(solution)/shard_map/psum | solution.py:131
  148.5 0.9 fusion.60
  150.2 1.0 fusion.56
  151.9 1.9 fusion.22
  153.8 47.2 %all-reduce.5.cloned.1.call-done = (bf16[256,1024]{1,0:T(8,128)(2,1)}, bf16[256,128]{1,0:T(8,128)(2,1)}, bf16[256,128]{1,0:T(8,128)(2,1)}, bf16[1024,256]{1,0:T(8,128)(2,1)}) async-done(((bf16[256,1024]{1,0:T(8,128)(2,1)}, bf16[256,128]{1,0:T(8,128)(2,1)}, bf16[256,128]{1,0:T(8,128)(2,1)}, bf16[1024,256]{1,0:T(8,128)(2,1)}), (bf16[256,1024]{1,0:T(8,128)(2,1)}, bf16[256,128]{1,0:T(8,128)(2,1)}, ...) | async-done | bytes 1179664 | tf_op jit(solution)/shard_map/psum | solution.py:140
  201.1 3.9 %fusion.4 = (f32[1024]{0:T(1024)S(1)}, bf16[1,1024,1024]{1,2,0:T(8,128)(2,1)}) fusion(bf16[1,1024,1024]{1,2,0:T(8,128)(2,1)} %copy.109, f32[1024]{0:T(1024)} %bitcast.268, bf16[256,1024]{1,0:T(8,128)(2,1)} %get-tuple-element.21, bf16[4096,256]{1,0:T(8,128)(2,1)S(1)} %copy-done, s32[]{:T(128)S(6)} %select_n.34), kind=kOutput, calls=%fused_computation.5 | convolution fusion | flops 542112768 | bytes 5251076 | tf_op jit(solution)/shard_map/dr,re->de/dot_general | solution.py:43
  204.9 4.0 %copy.83 = bf16[1,1024,1024]{2,1,0:T(8,128)(2,1)} copy(bf16[1,1024,1024]{1,2,0:T(8,128)(2,1)} %get-tuple-element.28) | data formatting | bytes 4194304
  211.3 2.1 convert_bitcast_fusion
  213.3 8.6 %psum.55 = f32[1024]{0:T(1024)S(1)} all-reduce(f32[1024]{0:T(1024)S(1)} %add_add_fusion), channel_id=1, replica_groups=mesh['pipe'=8,'tensor'=4,'dp'=4] {'tensor'}, use_global_device_ids=true, to_apply=%region_17.18 | all-reduce | flops 1024 | bytes 8192 | tf_op jit(solution)/shard_map/psum | solution.py:165
  222.0 8.7 %all_gather.3 = f32[4096]{0:T(1024)S(1)} all-gather(f32[1024]{0:T(1024)S(1)} %psum.55), channel_id=1, replica_groups=mesh['pipe'=8,'tensor'=4,'dp'=4] {'dp'}, dimensions={0}, use_global_device_ids=true | all-gather | bytes 20480 | tf_op jit(solution)/shard_map/all_gather | solution.py:165
  (129 shorter events, 13.9 us)
Async XLA Ops:
  7.2 141.4 %all-reduce.7.cloned.1.call-start = ((), (), s32[]{:S(2)}) async-start(), calls=%async_computation.1 | async-start | bytes 524288 | tf_op jit(solution)/shard_map/psum | solution.py:131
  8.9 36.2 %collective-permute-start = (bf16[256,256]{0,1:T(8,128)(2,1)}, bf16[256,256]{0,1:T(8,128)(2,1)}, u32[]{:S(2)}, u32[]{:S(2)}) collective-permute-start(bf16[256,256]{0,1:T(8,128)(2,1)} %bitcast), channel_id=1, source_target_pairs={{0,16},{16,32},{32,48},{48,64},{64,80},{80,96},{96,112},{1,17},{17... | collective-permute-start | bytes 393224 | tf_op jit(solution)/shard_map/ppermute | solution.py:18
  13.6 52.2 %collective-permute-start.1 = (bf16[256,256]{1,0:T(8,128)(2,1)}, bf16[256,256]{1,0:T(8,128)(2,1)}, u32[]{:S(2)}, u32[]{:S(2)}) collective-permute-start(bf16[256,256]{1,0:T(8,128)(2,1)} %bitcast.273), channel_id=1, source_target_pairs={{16,0},{32,16},{48,32},{64,48},{80,64},{96,80},{112,96},{17,1},{33... | collective-permute-start | bytes 393224 | tf_op jit(solution)/shard_map/ppermute | solution.py:18
  14.9 3.2 %copy-start.7 = (bf16[1,256,256]{2,1,0:T(8,128)(2,1)S(1)}, bf16[1,256,256]{2,1,0:T(8,128)(2,1)}, u32[]{:S(2)}) copy-start(bf16[1,256,256]{2,1,0:T(8,128)(2,1)} %param.15) | copy-start | bytes 393220
  14.9 4.8 %copy-start = (bf16[4096,256]{1,0:T(8,128)(2,1)S(1)}, bf16[4096,256]{1,0:T(8,128)(2,1)}, u32[]{:S(2)}) copy-start(bf16[4096,256]{1,0:T(8,128)(2,1)} %param.16) | copy-start | bytes 6291460
  14.9 4.8 %copy-start.36 = (f32[1,4096]{1,0:T(1,128)S(1)}, f32[1,4096]{1,0:T(1,128)}, u32[]{:S(2)}) copy-start(f32[1,4096]{1,0:T(1,128)} %param.17) | copy-start | bytes 49156
  18.0 13.3 %slice-start = ((s8[8388608]{0:T(1024)(128)(4,1)}), s8[4194304]{0:T(1024)(128)(4,1)S(1)}, s32[]{:S(2)}) async-start(s8[8388608]{0:T(1024)(128)(4,1)} %bitcast.271), calls=%async_computation.2 | async-start | bytes 8388608
  19.1 0.6 copy-start.46
  19.6 8.7 %copy-start.41 = (f32[256]{0:T(256)}, f32[256]{0:T(256)S(1)}, u32[]{:S(2)}) copy-start(f32[256]{0:T(256)S(1)} %add_rsqrt_fusion) | copy-start | bytes 3076
  19.6 6.0 %copy-start.39 = (bf16[1,4096,128]{2,1,0:T(8,128)(2,1)S(1)}, bf16[1,4096,128]{2,1,0:T(8,128)(2,1)}, u32[]{:S(2)}) copy-start(bf16[1,4096,128]{2,1,0:T(8,128)(2,1)} %param.19) | copy-start | bytes 3145732
  19.7 11.7 %slice-start.1 = ((s8[8388608]{0:T(1024)(128)(4,1)}), s8[4194304]{0:T(1024)(128)(4,1)S(1)}, s32[]{:S(2)}) async-start(s8[8388608]{0:T(1024)(128)(4,1)} %bitcast.271), calls=%async_computation.3 | async-start | bytes 8388608
  25.7 2.7 %copy-start.5 = (bf16[256,1024]{1,0:T(8,128)(2,1)}, bf16[256,1024]{1,0:T(8,128)(2,1)S(1)}, u32[]{:S(2)}) copy-start(bf16[256,1024]{1,0:T(8,128)(2,1)S(1)} %fusion.14) | copy-start | bytes 1572868
  27.1 4.3 %copy-start.23 = (bf16[256,128]{1,0:T(8,128)(2,1)}, bf16[256,128]{1,0:T(8,128)(2,1)S(1)}, u32[]{:S(2)}) copy-start(bf16[256,128]{1,0:T(8,128)(2,1)S(1)} %convolution_convert_fusion.6) | copy-start | bytes 196612
  27.1 2.2 copy-start.40
  29.3 5.2 %copy-start.27 = (f32[256,64]{0,1:T(8,128)}, f32[256,64]{0,1:T(8,128)S(1)}, u32[]{:S(2)}) copy-start(f32[256,64]{0,1:T(8,128)S(1)} %get-tuple-element.57) | copy-start | bytes 196612
  31.4 5.0 %copy-start.34 = (bf16[256,256]{1,0:T(8,128)(2,1)S(1)}, bf16[256,256]{1,0:T(8,128)(2,1)}, u32[]{:S(2)}) copy-start(bf16[256,256]{1,0:T(8,128)(2,1)} %param.11) | copy-start | bytes 393220
  38.7 14.2 %copy-start.1 = (f32[256,1024]{0,1:T(8,128)}, f32[256,1024]{0,1:T(8,128)S(1)}, u32[]{:S(2)}) copy-start(f32[256,1024]{0,1:T(8,128)S(1)} %copy.108) | copy-start | bytes 3145732
  43.3 6.1 %copy-start.24 = (bf16[256,128]{1,0:T(8,128)(2,1)S(1)}, bf16[256,128]{1,0:T(8,128)(2,1)}, u32[]{:S(2)}) copy-start(bf16[256,128]{1,0:T(8,128)(2,1)} %copy-done.23) | copy-start | bytes 196612
  46.0 3.5 %copy-start.15 = (bf16[256,256]{0,1:T(8,128)(2,1)}, bf16[256,256]{0,1:T(8,128)(2,1)S(1)}, u32[]{:S(2)}) copy-start(bf16[256,256]{0,1:T(8,128)(2,1)S(1)} %broadcast_select_fusion.1) | copy-start | bytes 393220
  47.1 2.3 copy-start.45
  52.9 1.4 copy-start.9
  55.9 5.2 %copy-start.3 = (f32[256,1024]{1,0:T(8,128)S(1)}, f32[256,1024]{1,0:T(8,128)}, u32[]{:S(2)}) copy-start(f32[256,1024]{1,0:T(8,128)} %fusion.13) | copy-start | bytes 3145732
  61.1 3.6 %copy-start.26 = (bf16[256,128,1]{0,1,2:T(8,128)(2,1)S(1)}, bf16[256,128,1]{0,1,2:T(8,128)(2,1)}, u32[]{:S(2)}) copy-start(bf16[256,128,1]{0,1,2:T(8,128)(2,1)} %get-tuple-element.53) | copy-start | bytes 196612
  61.1 3.6 %copy-start.28 = (pred[256,256]{0,1:T(8,128)(4,1)S(1)}, pred[256,256]{0,1:T(8,128)(4,1)}, u32[]{:S(2)}) copy-start(pred[256,256]{0,1:T(8,128)(4,1)} %iota_compare_fusion) | copy-start | bytes 196612
  64.8 1.0 copy-start.35
  64.8 2.6 %copy-start.16 = (bf16[1024,256]{1,0:T(8,128)(2,1)S(1)}, bf16[1024,256]{1,0:T(8,128)(2,1)}, u32[]{:S(2)}) copy-start(bf16[1024,256]{1,0:T(8,128)(2,1)} %fusion.17) | copy-start | bytes 1572868
  65.5 2.3 copy-start.32
  66.7 0.7 copy-start.11
  67.7 0.8 copy-start.17
  68.5 2.0 copy-start.19
  70.2 1.2 copy-start.2
  70.2 1.5 copy-start.4
  80.9 1.3 copy-start.6
  80.9 1.3 copy-start.44
  86.2 3.5 %copy-start.10 = (f32[256,128]{0,1:T(8,128)S(1)}, f32[256,128]{0,1:T(8,128)}, u32[]{:S(2)}) copy-start(f32[256,128]{0,1:T(8,128)} %get-tuple-element.54) | copy-start | bytes 393220
  96.9 4.1 %copy-start.25 = (bf16[256,128]{1,0:T(8,128)(2,1)S(1)}, bf16[256,128]{1,0:T(8,128)(2,1)}, u32[]{:S(2)}) copy-start(bf16[256,128]{1,0:T(8,128)(2,1)} %copy-done.23) | copy-start | bytes 196612
  98.5 2.7 %copy-start.18 = (bf16[256,1024]{1,0:T(8,128)(2,1)S(1)}, bf16[256,1024]{1,0:T(8,128)(2,1)}, u32[]{:S(2)}) copy-start(bf16[256,1024]{1,0:T(8,128)(2,1)} %copy-done.17) | copy-start | bytes 1572868
  98.5 2.8 %copy-start.12 = (bf16[256,256]{1,0:T(8,128)(2,1)S(1)}, bf16[256,256]{1,0:T(8,128)(2,1)}, u32[]{:S(2)}) copy-start(bf16[256,256]{1,0:T(8,128)(2,1)} %copy-done.11) | copy-start | bytes 393220
  98.5 2.8 %copy-start.14 = (bf16[128,8,256]{2,0,1:T(8,128)(2,1)S(1)}, bf16[128,8,256]{2,0,1:T(8,128)(2,1)}, u32[]{:S(2)}) copy-start(bf16[128,8,256]{2,0,1:T(8,128)(2,1)} %convolution_convert_fusion.1) | copy-start | bytes 1572868
  101.0 1.5 copy-start.8
  101.3 2.2 copy-start.33
  102.9 0.6 copy-start.29
  104.4 96.7 %all-reduce.5.cloned.1.call-start = ((), (), s32[]{:S(2)}) async-start(), calls=%async_computation | async-start | bytes 2359296 | tf_op jit(solution)/shard_map/psum | solution.py:140
  104.7 1.5 copy-start.30
  104.7 1.5 copy-start.42
  115.4 33.1 %copy-start.21 = (f32[256,256]{0,1:T(8,128)S(1)}, f32[256,256]{0,1:T(8,128)}, u32[]{:S(2)}) copy-start(f32[256,256]{0,1:T(8,128)} %get-tuple-element.61) | copy-start | bytes 786436
  115.4 36.5 %copy-start.13 = (bf16[256,256]{1,0:T(8,128)(2,1)S(1)}, bf16[256,256]{1,0:T(8,128)(2,1)}, u32[]{:S(2)}) copy-start(bf16[256,256]{1,0:T(8,128)(2,1)} %copy-done.11) | copy-start | bytes 393220
  115.4 36.5 %copy-start.20 = (f32[256,256]{1,0:T(8,128)S(1)}, f32[256,256]{1,0:T(8,128)}, u32[]{:S(2)}) copy-start(f32[256,256]{1,0:T(8,128)} %get-tuple-element.59) | copy-start | bytes 786436
  204.9 4.0 %copy-start.22 = (bf16[1,1024,128]{1,2,0:T(8,128)(2,1)S(1)}, bf16[1,1024,128]{1,2,0:T(8,128)(2,1)}, u32[]{:S(2)}) copy-start(bf16[1,1024,128]{1,2,0:T(8,128)(2,1)} %copy.110) | copy-start | bytes 786436
  204.9 4.0 %copy-start.38 = (bf16[256,128]{1,0:T(8,128)(2,1)S(1)}, bf16[256,128]{1,0:T(8,128)(2,1)}, u32[]{:S(2)}) copy-start(bf16[256,128]{1,0:T(8,128)(2,1)} %get-tuple-element.22) | copy-start | bytes 196612
  204.9 4.0 %copy-start.43 = (f32[1,1024]{1,0:T(1,128)S(1)}, f32[1,1024]{1,0:T(1,128)}, u32[]{:S(2)}) copy-start(f32[1,1024]{1,0:T(1,128)} %constant_dynamic-slice_fusion.3) | copy-start | bytes 12292
  204.9 5.2 %copy-start.37 = (bf16[256,128]{1,0:T(8,128)(2,1)S(1)}, bf16[256,128]{1,0:T(8,128)(2,1)}, u32[]{:S(2)}) copy-start(bf16[256,128]{1,0:T(8,128)(2,1)} %get-tuple-element.23) | copy-start | bytes 196612
  208.9 2.4 copy-start.31
Sparse Core Ops, SparseCore 0:
  104.5 43.9 all-reduce.6
  151.5 49.4 all-reduce.4
where the time goes:
time: 239 us; the launch traced here: 238 us
  waiting for transfers between devices  76 us (32%)
  matrix products  54.3 us (23%)
  local copies, waits for them, and re-layouts  46.1 us (19%)
  other arithmetic  23.5 us (10%)
  blocking collectives  17.3 us (7%)
  between operations  14.6 us (6%)
  starting transfers between devices  6.27 us (3%)
    dot_general x31, matrix products, dot(): return jnp.einsum(spec, a, b, preferred_element_type=F32)  50.3 us
    psum x1, waiting for transfers between devices, body(): lax.psum((query_term.astype(BF16), key_term.astype(BF16), value_term.asty...  47.2 us
    psum x1, waiting for transfers between devices, body(): lax.psum((forward_part.astype(BF16), backward_part.astype(BF16)), 'tensor')  28.7 us
    unnamed x109, local copies, waits for them, and re-layouts  20.2 us
    all_gather x1, blocking collectives, body(): grad_gain = lax.all_gather(lax.psum(gain_part, 'tensor'), 'dp', tiled=True)  8.66 us
    psum x1, blocking collectives, body(): grad_gain = lax.all_gather(lax.psum(gain_part, 'tensor'), 'dp', tiled=True)  8.64 us
    ppermute x2, starting transfers between devices, shifted(): return lax.ppermute(x, axis, pairs)  5.97 us
    mul x2, local copies, waits for them, and re-layouts, apply_rope(): rotate_half(values) * sine_table[:, None, :]  5.22 us
  transfers between devices with their start and end apart: 4, of which 2 were waited for; matrix products, arithmetic and copies ran while one was open for 30% of the time, Pallas kernels for 0%

commit v1 on v0

v1 whole, which is shorter than its diff:
```python
import functools
import math

import jax
import jax.numpy as jnp
import numpy as np
from jax import lax
from jax.experimental import pallas as pl
from jax.experimental.pallas import tpu as pltpu
from jax.sharding import PartitionSpec as P

MESH = pl.DeviceIdType.MESH
HD = 128
HALF = HD // 2
EPSILON = 1e-05
ROPE_BASE = 500000.0
BF16 = jnp.bfloat16
F32 = jnp.float32
SCALE = 1.0 / math.sqrt(HD)
LOG2E = math.log2(math.e)
CHUNK = 512


def rope_tables(length):
    exponent = (np.float32(-2.0) * np.arange(HALF, dtype=np.float32)) / np.float32(HD)
    frequency = np.float32(ROPE_BASE) ** exponent
    angles = frequency[:, None] * np.arange(length, dtype=np.float32)[None, :]
    return np.cos(angles).astype(np.float32), np.sin(angles).astype(np.float32)


def nn(a, b):
    return jnp.dot(a, b, preferred_element_type=F32)


def nt(a, b):
    return lax.dot_general(a, b, (((1,), (1,)), ((), ())), preferred_element_type=F32)


def rope(x, cos, sin):
    x1, x2 = x[:HALF], x[HALF:]
    return jnp.concatenate([x1 * cos - x2 * sin, x2 * cos + x1 * sin], axis=0)


def undo_rope(x, cos, sin):
    x1, x2 = x[:HALF], x[HALF:]
    return jnp.concatenate([x1 * cos + x2 * sin, x2 * cos - x1 * sin], axis=0)


def main_kernel(
    sizes,
    new_coeffs,
    loss_grad,
    sent_forward,
    sent_backward,
    stashed,
    basis,
    gain,
    w_query,
    w_key,
    w_value,
    w_output,
    cos_in,
    sin_in,
    mn_out,
    fb_out,
    gg_out,
    s_v,
    st_v,
    gain_v,
    cos_v,
    sin_v,
    wq_v,
    wk_v,
    wv_v,
    wo_v,
    gw_acc,
    ws_acc,
    gram_acc,
    gw,
    gwt,
    ws,
    wst,
    gram3,
    cb,
    gb,
    cf,
    mt_acc,
    n_acc,
    dt,
    o_v,
    u_own,
    part,
    pair_send,
    pair_recv,
    rs_send,
    rs_recv,
    shard_v,
    m_v,
    n_v,
    kv_recv,
    gg_part,
    gg_recv,
    load_sem,
    in_sem,
    in_send,
    relay_send,
    pair_sem,
    rs_ssem,
    rs_rsem,
    ag_ssem,
    ag_rsem,
    own_sem,
    m_ssem,
    m_rsem,
    gg_ssem,
    gg_rsem,
):
    pipes, tensors, width, rank, heads, length = sizes
    eq = heads * HD
    p = lax.axis_index("pipe")
    z = lax.axis_index("tensor")
    n = lax.axis_index("dp")
    h = n // 2
    k = n % 2
    partner = 2 * h + 1 - k
    across = 2 * (1 - h) + k
    after = lax.rem(p + 1, pipes)
    before = lax.rem(p + pipes - 1, pipes)
    others = [(dz, dn) for dz in range(tensors) for dn in range(4) if (dz, dn) != (0, 0)]
    others = [
        (lax.rem(z + dz, tensors), lax.rem(n + dn, 4)) for dz, dn in others
    ]

    barrier = pltpu.get_barrier_semaphore()
    for oz, on in others:
        pl.semaphore_signal(barrier, inc=1, device_id=(p, oz, on), device_id_type=MESH)
    for op, on in ((before, n), (after, n), (after, across)):
        pl.semaphore_signal(barrier, inc=1, device_id=(op, z, on), device_id_type=MESH)

    steps = width // CHUNK
    col = pl.multiple_of(k * eq, HD)

    def loads(i):
        rows = pl.ds(pl.multiple_of(i * CHUNK, CHUNK), CHUNK)
        return (
            pltpu.make_async_copy(basis.at[rows, :], s_v.at[rows, :], load_sem.at[i, 0]),
            pltpu.make_async_copy(
                w_query.at[rows, pl.ds(col, eq)], wq_v.at[rows, :], load_sem.at[i, 1]
            ),
            pltpu.make_async_copy(w_key.at[rows, :], wk_v.at[rows, :], load_sem.at[i, 2]),
            pltpu.make_async_copy(w_value.at[rows, :], wv_v.at[rows, :], load_sem.at[i, 3]),
            pltpu.make_async_copy(
                w_output.at[pl.ds(col, eq), rows], wo_v.at[:, rows], load_sem.at[i, 4]
            ),
        )

    small = (
        pltpu.make_async_copy(gain, gain_v, load_sem.at[steps, 0]),
        pltpu.make_async_copy(cos_in, cos_v, load_sem.at[steps, 1]),
        pltpu.make_async_copy(sin_in, sin_v, load_sem.at[steps, 2]),
        pltpu.make_async_copy(stashed, cb.at[0], load_sem.at[steps, 3]),
    )
    small[0].start()
    for i in range(steps):
        for copy in loads(i):
            copy.start()
    for copy in small[1:]:
        copy.start()

    gw_acc[...] = jnp.zeros_like(gw_acc)
    ws_acc[...] = jnp.zeros_like(ws_acc)
    gram_acc[...] = jnp.zeros_like(gram_acc)
    small[0].wait()

    def weight_step(i, _):
        rows = pl.ds(pl.multiple_of(i * CHUNK, CHUNK), CHUNK)
        copies = loads(i)
        copies[0].wait()
        s = s_v[rows, :]
        st = s.T
        st_v[:, rows] = st
        gram_acc[...] += nn(st, s)
        stg = (st.astype(F32) * gain_v[:, rows]).astype(BF16)
        copies[1].wait()
        gw_acc[:, :eq] += nn(stg, wq_v[rows, :])
        copies[2].wait()
        gw_acc[:, eq : eq + HD] += nn(stg, wk_v[rows, :])
        copies[3].wait()
        gw_acc[:, eq + HD :] += nn(stg, wv_v[rows, :])
        copies[4].wait()
        ws_acc[...] += nn(wo_v[:, rows], s)
        return 0

    def remote(src, dst, ssem, rsem, device):
        return pltpu.make_async_remote_copy(
            src_ref=src,
            dst_ref=dst,
            send_sem=ssem,
            recv_sem=rsem,
            device_id=device,
            device_id_type=MESH,
        )

    def input_copies(grads, coeffs):
        return (
            remote(grads, gb.at[0], in_send.at[0], in_sem.at[0], (before, z, n)),
            remote(coeffs, cf.at[0], in_send.at[1], in_sem.at[1], (after, z, n)),
            remote(grads, gb.at[2], in_send.at[2], in_sem.at[2], (before, z, across)),
        )

    stash_pair = remote(stashed, cb.at[1], in_send.at[3], in_sem.at[3], (p, z, partner))
    stash_across = remote(stashed, cb.at[2], in_send.at[4], in_sem.at[4], (p, z, across))
    sends = input_copies(sent_backward, sent_forward)
    edge_sends = input_copies(loss_grad, new_coeffs)

    pl.semaphore_wait(barrier, len(others) + 3)

    @pl.when(p == 0)
    def _():
        edge_sends[0].start()

    @pl.when(p != 0)
    def _():
        sends[0].start()

    stash_pair.start()

    @pl.when(p == pipes - 1)
    def _():
        edge_sends[1].start()

    @pl.when(p != pipes - 1)
    def _():
        sends[1].start()

    @pl.when(p == 0)
    def _():
        edge_sends[2].start()

    @pl.when(p != 0)
    def _():
        sends[2].start()

    stash_across.start()

    lax.fori_loop(0, steps, weight_step, 0)

    gw_value = gw_acc[...].astype(BF16)
    gw[...] = gw_value
    gwt[...] = gw_value.T
    ws_value = ws_acc[...].astype(BF16)
    ws[...] = ws_value
    wst[...] = ws_value.T
    gram = gram_acc[...]
    first = gram.astype(BF16)
    rest = gram - first.astype(F32)
    second = rest.astype(BF16)
    gram3[0] = first
    gram3[1] = second
    gram3[2] = (rest - second.astype(F32)).astype(BF16)
    for copy in small[1:]:
        copy.wait()

    cos = cos_v[...]
    sin = sin_v[...]
    shape = (length, length)
    causal = lax.broadcasted_iota(jnp.int32, shape, 0) <= lax.broadcasted_iota(
        jnp.int32, shape, 1
    )

    def project(c):
        ct = c.T
        ut = nn(gram3[0], ct) + nn(gram3[1], ct) + nn(gram3[2], ct)
        square = jnp.sum(ut * ct.astype(F32), axis=0, keepdims=True) * (1.0 / width)
        inverse = lax.rsqrt(jnp.maximum(square, 0.0) + EPSILON)
        qkv = nn(gwt[...], ct)
        queries = [
            rope(qkv[i * HD : (i + 1) * HD] * (inverse * (SCALE * LOG2E)), cos, sin).astype(BF16)
            for i in range(heads)
        ]
        keys = rope(qkv[eq : eq + HD] * inverse, cos, sin).astype(BF16)
        values = (qkv[eq + HD :] * inverse).astype(BF16)
        return ct, ut, inverse, queries, keys, values

    def softmax(keys_rows, query):
        scores = jnp.where(causal, nn(keys_rows, query), -1e30)
        powers = jnp.exp2(scores - jnp.max(scores, axis=0, keepdims=True))
        return powers.astype(BF16), powers, 1.0 / jnp.sum(powers, axis=0, keepdims=True)

    def backward(slot, initial, own):
        c = cb[slot]
        g = gb[slot]
        ct, ut, inverse, queries, keys, values = project(c)
        keys_rows = keys.T
        values_rows = values.T
        grads = nt(ws[...], g)
        dk = jnp.zeros((HD, length), F32)
        dv = jnp.zeros((HD, length), F32)
        for i in range(heads):
            rows = slice(i * HD, (i + 1) * HD)
            low, powers, weight = softmax(keys_rows, queries[i])
            out = nn(values, low) * weight
            o_v[rows, :] = out.astype(BF16)
            grad = (grads[rows] * weight).astype(BF16)
            through = nn(values_rows, grad)
            centre = jnp.sum(grad.astype(F32) * out, axis=0, keepdims=True)
            ds = (powers * (through - centre)).astype(BF16)
            dq = undo_rope(nn(keys, ds), cos, sin)
            dt[rows, :] = (dq * (inverse * SCALE)).astype(BF16)
            dk = dk + nt(queries[i], ds)
            dv = dv + nt(grad, low)
        dt[eq : eq + HD, :] = (undo_rope(dk, cos, sin) * (inverse * (1.0 / LOG2E))).astype(BF16)
        dt[eq + HD :, :] = (dv * inverse).astype(BF16)
        d = dt[...]
        mt = nn(d, c)
        nv = nn(o_v[...], g)
        if initial:
            mt_acc[...] = mt
            n_acc[...] = nv
        else:
            mt_acc[...] += mt
            n_acc[...] += nv
        if not own:
            return None
        back = nn(gw[...], d)
        middle = jnp.sum(back * ct.astype(F32), axis=0, keepdims=True)
        return back - ut * (inverse * inverse * middle * (1.0 / width))

    def forward(slot):
        ct, ut, inverse, queries, keys, values = project(cf[slot])
        keys_rows = keys.T
        for i in range(heads):
            low, _, weight = softmax(keys_rows, queries[i])
            o_v[i * HD : (i + 1) * HD, :] = (nn(values, low) * weight).astype(BF16)
        return ut, nn(wst[...], o_v[...])

    shard = rank // tensors
    mine = pl.ds(pl.multiple_of(z * shard, shard), shard)

    def pair_copy(i):
        return remote(
            pair_send.at[i], pair_recv.at[i], pair_sem.at[i, 0], pair_sem.at[i, 1], (p, z, partner)
        )

    def scatter_copies(i):
        out = []
        for dz in range(1, tensors):
            to = lax.rem(z + dz, tensors)
            rows = pl.ds(pl.multiple_of(to * shard, shard), shard)
            out.append(
                remote(
                    rs_send.at[i, rows, :],
                    rs_recv.at[i, dz],
                    rs_ssem.at[i, dz],
                    rs_rsem.at[i, dz],
                    (p, to, n),
                )
            )
        return out

    def gather_copies(i):
        out = []
        for dz in range(1, tensors):
            to = lax.rem(z + dz, tensors)
            out.append(
                remote(
                    shard_v.at[i], fb_out.at[i, mine, :], ag_ssem.at[i, dz], ag_rsem.at[i, dz], (p, to, n)
                )
            )
        return out

    def own_copy(i):
        return pltpu.make_async_copy(shard_v.at[i], fb_out.at[i, mine, :], own_sem.at[i])

    def start_pair(i, value):
        pair_send[i] = value.astype(BF16)
        pair_copy(i).start()

    def start_scatter(i):
        pair_copy(i).wait_recv()
        total = part[i] + pair_recv[i].astype(F32)
        part[i] = total
        rs_send[i] = total.astype(BF16)
        for copy in scatter_copies(i):
            copy.start()

    def start_gather(i, extra):
        total = part[i, mine, :] + extra
        for dz, copy in enumerate(scatter_copies(i), 1):
            copy.wait_recv()
            total = total + rs_recv[i, dz].astype(F32)
        shard_v[i] = total.astype(BF16)
        for copy in gather_copies(i):
            copy.start()
        own_copy(i).start()

    relay_g0 = remote(gb.at[0], gb.at[1], relay_send.at[0], in_sem.at[5], (p, z, partner))
    relay_cf = remote(cf.at[0], cf.at[1], relay_send.at[1], in_sem.at[6], (p, z, partner))
    relay_g2 = remote(gb.at[2], gb.at[3], relay_send.at[2], in_sem.at[7], (p, z, partner))
    relay_cb = remote(cb.at[2], cb.at[3], relay_send.at[3], in_sem.at[8], (p, z, partner))

    sends[0].wait_recv()
    relay_g0.start()
    part[1] = backward(0, True, True)

    sends[1].wait_recv()
    relay_cf.start()
    stash_pair.wait_recv()
    relay_g0.wait_recv()
    start_pair(1, backward(1, False, True))

    ut, value = forward(0)
    u_own[...] = ut[...]
    part[0] = value

    sends[2].wait_recv()
    relay_g2.start()
    stash_across.wait_recv()
    relay_cb.start()
    start_scatter(1)
    relay_cf.wait_recv()
    _, value = forward(1)
    start_pair(0, value)

    own_g = gb[0]
    lift = (
        nt(gram3[0, mine, :], own_g) + nt(gram3[1, mine, :], own_g) + nt(gram3[2, mine, :], own_g)
    )
    start_gather(1, lift)
    backward(2, False, False)

    start_scatter(0)
    relay_g2.wait_recv()
    relay_cb.wait_recv()
    backward(3, False, False)

    start_gather(0, u_own[mine, :])

    m_value = mt_acc[...].astype(BF16)
    m_v[...] = m_value
    n_v[...] = n_acc[...].astype(BF16)
    kv_rows = pl.ds(2 * eq, 2 * HD)
    q_rows = pl.ds(pl.multiple_of(k * eq, eq), eq)
    n_rows = pl.ds(pl.multiple_of(2 * eq + 2 * HD + k * eq, HD), eq)
    peer = (p, z, partner)
    exchange = (
        remote(mt_acc.at[pl.ds(eq, 2 * HD), :], kv_recv, m_ssem.at[0], m_rsem.at[0], peer),
        remote(m_v.at[pl.ds(0, eq), :], mn_out.at[q_rows, :], m_ssem.at[1], m_rsem.at[1], peer),
        remote(n_v, mn_out.at[n_rows, :], m_ssem.at[2], m_rsem.at[2], peer),
    )
    keep = (
        pltpu.make_async_copy(m_v.at[pl.ds(0, eq), :], mn_out.at[q_rows, :], own_sem.at[2]),
        pltpu.make_async_copy(n_v, mn_out.at[n_rows, :], own_sem.at[3]),
    )
    for copy in exchange + keep:
        copy.start()

    m_nat = m_value.T
    half_width = width // 2
    block = half_width // 8
    for i in range(8):
        rows = pl.ds(pl.multiple_of(h * half_width + i * block, block), block)
        lifted = (
            nt(m_nat[:, :eq], wq_v[rows, :])
            + nt(m_nat[:, eq : eq + HD], wk_v[rows, :])
            + nt(m_nat[:, eq + HD :], wv_v[rows, :])
        )
        gg_part[i : i + 1, :] = jnp.sum(lifted * st_v[:, rows].astype(F32), axis=0, keepdims=True)
    me = z * 4 + n
    gg_copies = [
        remote(gg_part, gg_recv.at[me], gg_ssem.at[i], gg_rsem.at[me], (p, oz, on))
        for i, (oz, on) in enumerate(others)
    ]
    for copy in gg_copies:
        copy.start()

    exchange[0].wait_recv()
    kv_total = mt_acc[eq:, :] + kv_recv[...]
    m_v[eq:, :] = kv_total.astype(BF16)
    kv_keep = pltpu.make_async_copy(
        m_v.at[pl.ds(eq, 2 * HD), :], mn_out.at[kv_rows, :], own_sem.at[4]
    )
    kv_keep.start()

    gg_recv[me] = gg_part[...]
    for oz, on in others:
        it = oz * 4 + on
        remote(gg_part, gg_recv.at[it], gg_ssem.at[0], gg_rsem.at[it], (p, oz, on)).wait_recv()
    for hh in range(2):
        total = gg_recv[2 * hh] + gg_recv[2 * hh + 1]
        for zz in range(1, tensors):
            total = total + gg_recv[4 * zz + 2 * hh] + gg_recv[4 * zz + 2 * hh + 1]
        gg_out[8 * hh : 8 * hh + 8, :] = total

    for copy in exchange[1:]:
        copy.wait_recv()
    for copy in exchange:
        copy.wait_send()
    for copy in keep + (kv_keep,):
        copy.wait()
    for copy in gg_copies:
        copy.wait_send()
    for i in range(2):
        own_copy(i).wait()
        pair_copy(i).wait_send()
        for copy in scatter_copies(i):
            copy.wait_send()
        for copy in gather_copies(i):
            copy.wait()
    for copy in sends + (stash_pair, stash_across, relay_g0, relay_cf, relay_g2, relay_cb):
        copy.wait_send()


def slice_kernel(
    sizes,
    mn,
    fb,
    gg,
    basis,
    gain,
    forward_out,
    backward_out,
    gq_out,
    gk_out,
    gv_out,
    go_out,
    gain_out,
    mn_v,
    s_v,
    gain_v,
    gq_v,
    go_v,
    load_sem,
    out_sem,
):
    rows_own, eq, block = sizes
    n = lax.axis_index("dp")
    own = pl.ds(pl.multiple_of(n * rows_own, rows_own), rows_own)
    copies = (
        pltpu.make_async_copy(basis.at[own, :], s_v, load_sem.at[0]),
        pltpu.make_async_copy(gain.at[:, own], gain_v, load_sem.at[1]),
        pltpu.make_async_copy(mn, mn_v, load_sem.at[2]),
    )
    for copy in copies:
        copy.start()
    forward_out[...] = fb[0].T
    backward_out[...] = fb[1].T
    wide = gg.shape[1]
    for i in range(gg.shape[0]):
        gain_out[:, i * wide : (i + 1) * wide] = gg[i : i + 1, :]
    for copy in copies:
        copy.wait()
    gain_cols = jnp.broadcast_to(gain_v[...], (HD, rows_own)).T
    n_at = eq + 2 * HD

    outs = []
    for i in range(rows_own // block):
        rows = slice(i * block, (i + 1) * block)
        s = s_v[rows, :]
        scale = gain_cols[rows, :]
        for j in range(eq // HD // 2):
            cols = slice(2 * j * HD, 2 * (j + 1) * HD)
            value = nt(s, mn_v[cols, :])
            gq_v[rows, cols] = (value * jnp.concatenate([scale, scale], axis=1)).astype(BF16)
        copy = pltpu.make_async_copy(gq_v.at[rows, :], gq_out.at[rows, :], out_sem.at[i])
        copy.start()
        outs.append(copy)
        value = nt(s, mn_v[eq:n_at, :])
        gk_out[rows, :] = (value[:, :HD] * scale).astype(BF16)
        gv_out[rows, :] = (value[:, HD:] * scale).astype(BF16)
    s = s_v[...]
    for i in range(eq // block):
        rows = slice(i * block, (i + 1) * block)
        go_v[rows, :] = nt(mn_v[n_at + i * block : n_at + (i + 1) * block, :], s).astype(BF16)
        copy = pltpu.make_async_copy(
            go_v.at[rows, :], go_out.at[rows, :], out_sem.at[rows_own // block + i]
        )
        copy.start()
        outs.append(copy)
    for copy in outs:
        copy.wait()


def body(
    new_coeffs,
    loss_grad,
    sent_forward,
    sent_backward,
    stashed,
    subspace,
    norm_gain,
    w_query,
    w_key,
    w_value,
    w_output,
):
    pipes = lax.axis_size("pipe")
    tensors = lax.axis_size("tensor")
    parts = lax.axis_size("dp")
    length = new_coeffs.shape[0]
    width, rank = subspace.shape
    both = w_query.shape[2]
    eq = both // 2
    heads = eq // HD
    cos, sin = rope_tables(length)
    any_spec = pl.BlockSpec(memory_space=pl.ANY)
    vmem_spec = pl.BlockSpec(memory_space=pltpu.VMEM)
    steps = width // CHUNK
    total = 2 * both + 2 * HD
    shard = rank // tensors
    dma = pltpu.SemaphoreType.DMA
    square = (rank, rank)
    mn, fb, gg = pl.pallas_call(
        functools.partial(main_kernel, (pipes, tensors, width, rank, heads, length)),
        out_shape=(
            jax.ShapeDtypeStruct((total, rank), BF16),
            jax.ShapeDtypeStruct((2, rank, length), BF16),
            jax.ShapeDtypeStruct((16, width // 16), F32),
        ),
        in_specs=[any_spec] * 13,
        out_specs=(any_spec, any_spec, vmem_spec),
        scratch_shapes=[
            pltpu.VMEM((width, rank), BF16),
            pltpu.VMEM((rank, width), BF16),
            pltpu.VMEM((1, width), F32),
            pltpu.VMEM((HALF, length), F32),
            pltpu.VMEM((HALF, length), F32),
            pltpu.VMEM((width, eq), BF16),
            pltpu.VMEM((width, HD), BF16),
            pltpu.VMEM((width, HD), BF16),
            pltpu.VMEM((eq, width), BF16),
            pltpu.VMEM((rank, eq + 2 * HD), F32),
            pltpu.VMEM((eq, rank), F32),
            pltpu.VMEM(square, F32),
            pltpu.VMEM((rank, eq + 2 * HD), BF16),
            pltpu.VMEM((eq + 2 * HD, rank), BF16),
            pltpu.VMEM((eq, rank), BF16),
            pltpu.VMEM((rank, eq), BF16),
            pltpu.VMEM((3, rank, rank), BF16),
            pltpu.VMEM((4, length, rank), BF16),
            pltpu.VMEM((4, length, rank), BF16),
            pltpu.VMEM((2, length, rank), BF16),
            pltpu.VMEM((eq + 2 * HD, rank), F32),
            pltpu.VMEM((eq, rank), F32),
            pltpu.VMEM((eq + 2 * HD, length), BF16),
            pltpu.VMEM((eq, length), BF16),
            pltpu.VMEM((rank, length), F32),
            pltpu.VMEM((2, rank, length), F32),
            pltpu.VMEM((2, rank, length), BF16),
            pltpu.VMEM((2, rank, length), BF16),
            pltpu.VMEM((2, rank, length), BF16),
            pltpu.VMEM((2, tensors, shard, length), BF16),
            pltpu.VMEM((2, shard, length), BF16),
            pltpu.VMEM((eq + 2 * HD, rank), BF16),
            pltpu.VMEM((eq, rank), BF16),
            pltpu.VMEM((2 * HD, rank), F32),
            pltpu.VMEM((8, width // 16), F32),
            pltpu.VMEM((4 * tensors, 8, width // 16), F32),
            dma((steps + 1, 5)),
            dma((9,)),
            dma((5,)),
            dma((4,)),
            dma((2, 2)),
            dma((2, tensors)),
            dma((2, tensors)),
            dma((2, tensors)),
            dma((2, tensors)),
            dma((5,)),
            dma((3,)),
            dma((3,)),
            dma((4 * tensors,)),
            dma((4 * tensors,)),
        ],
        compiler_params=pltpu.CompilerParams(
            collective_id=0, has_side_effects=True, vmem_limit_bytes=56 * 1024 * 1024
        ),
    )(
        new_coeffs,
        loss_grad,
        sent_forward[0],
        sent_backward[0],
        stashed[0],
        subspace,
        norm_gain,
        w_query[0],
        w_key[0],
        w_value[0],
        w_output[0],
        cos,
        sin,
    )
    rows_own = width // parts
    block = 256
    outs = pl.pallas_call(
        functools.partial(slice_kernel, (rows_own, both, block)),
        out_shape=(
            jax.ShapeDtypeStruct((length, rank), BF16),
            jax.ShapeDtypeStruct((length, rank), BF16),
            jax.ShapeDtypeStruct((rows_own, both), BF16),
            jax.ShapeDtypeStruct((rows_own, HD), BF16),
            jax.ShapeDtypeStruct((rows_own, HD), BF16),
            jax.ShapeDtypeStruct((both, rows_own), BF16),
            jax.ShapeDtypeStruct((1, width), F32),
        ),
        in_specs=[any_spec, vmem_spec, vmem_spec, any_spec, any_spec],
        out_specs=(vmem_spec, vmem_spec, any_spec, vmem_spec, vmem_spec, any_spec, vmem_spec),
        scratch_shapes=[
            pltpu.VMEM((total, rank), BF16),
            pltpu.VMEM((rows_own, rank), BF16),
            pltpu.VMEM((1, rows_own), F32),
            pltpu.VMEM((rows_own, both), BF16),
            pltpu.VMEM((both, rows_own), BF16),
            dma((3,)),
            dma((rows_own // block + both // block,)),
        ],
        compiler_params=pltpu.CompilerParams(vmem_limit_bytes=56 * 1024 * 1024),
    )(mn, fb, gg, subspace, norm_gain)
    forward_out, backward_out, gq, gk, gv, go, gain_row = outs
    return (
        forward_out[None],
        backward_out[None],
        gq[None],
        gk[None],
        gv[None],
        go[None],
        gain_row,
    )


def solution(mesh):
    return jax.shard_map(
        body,
        mesh=mesh,
        in_specs=(
            P("dp", None),
            P("dp", None),
            P("pipe", "dp", None),
            P("pipe", "dp", None),
            P("pipe", "dp", None),
            P(),
            P("pipe", None),
            P("pipe", None, "tensor"),
            P("pipe", None, "tensor"),
            P("pipe", None, "tensor"),
            P("pipe", "tensor", None),
        ),
        out_specs=(
            P("pipe", "dp", None),
            P("pipe", "dp", None),
            P("pipe", "dp", "tensor"),
            P("pipe", "dp", "tensor"),
            P("pipe", "dp", "tensor"),
            P("pipe", "tensor", "dp"),
            P("pipe", None),
        ),
        check_vma=False,
    )
```

time: 239 us -> 54.8 us (0.23)
  waiting for transfers between devices: 76 us -> 0 us
  matrix products: 54.3 us -> 0 us
  Pallas kernels: 0 us -> 53.8 us
  local copies, waits for them, and re-layouts: 46.1 us -> 0 us
  other arithmetic: 23.5 us -> 0 us
  blocking collectives: 17.3 us -> 0 us
  between operations: 14.6 us -> 0.8 us
  starting transfers between devices: 6.27 us -> 0 us
    psum x2 -> x0, waiting for transfers between devices: 76 us -> none  [the longest x1 47.2 us: body(): lax.psum((query_term.astype(BF16), key_term.astype(BF16), value_term.asty...]
    dot_general x34 -> x0, matrix products: 54.3 us -> none  [the longest x31 50.3 us: dot(): return jnp.einsum(spec, a, b, preferred_element_type=F32)]
    pallas_call x0 -> x2, Pallas kernels: none -> 53.8 us  [the longest x1 48 us: body(): pl.pallas_call(functools.partial(main_kernel, (pipes, tensors, width, ran...]
    unnamed x109 -> x0, local copies, waits for them, and re-layouts: 20.2 us -> none
    mul x5 -> x0, local copies, waits for them, and re-layouts: 12.4 us -> none  [the longest x2 5.22 us: apply_rope(): rotate_half(values) * sine_table[:, None, :]]
    all_gather x1 -> x0, blocking collectives: 8.66 us -> none  [body(): grad_gain = lax.all_gather(lax.psum(gain_part, 'tensor'), 'dp', tiled=True)]
    psum x1 -> x0, blocking collectives: 8.64 us -> none  [body(): grad_gain = lax.all_gather(lax.psum(gain_part, 'tensor'), 'dp', tiled=True)]
    ppermute x2 -> x0, starting transfers between devices: 5.97 us -> none  [shifted(): return lax.ppermute(x, axis, pairs)]
  transfers between devices with their start and end apart: 4 -> 0, of which waited for: 2 -> 0; matrix products, arithmetic and copies ran while one was open for 30% -> 0% of each run, Pallas kernels for 0% -> 0%
where the time goes in v1:
time: 54.8 us; the launch traced here: 54.6 us
  Pallas kernels  53.8 us (98%)
  between operations  0.8 us (1%)
    pallas_call x1, Pallas kernels, body(): pl.pallas_call(functools.partial(main_kernel, (pipes, tensors, width, ran...  48 us
    pallas_call x1, Pallas kernels, body(): pl.pallas_call(functools.partial(slice_kernel, (rows_own, both, block)),...  5.77 us

profile of v1, /device:TPU:1, one launch (start us, length us, event | category | flops | bytes accessed | tf_op | source)
XLA Modules:
  0.0 54.6 jit_solution(14034385511785511358)
XLA Ops:
  0.6 48.0 %shard_map.180 = (bf16[2304,256]{1,0:T(8,128)(2,1)}, bf16[2,256,256]{2,1,0:T(8,128)(2,1)}, f32[16,256]{1,0:T(8,128)}) custom-call(bf16[256,256]{1,0:T(8,128)(2,1)} %new_coeffs.1, bf16[256,256]{1,0:T(8,128)(2,1)} %loss_grad.1, bf16[256,256]{1,0:T(8,128)(2,1)} %bitcast.17, bf16[256,256]{1,0:T(8,128)(2,1)} %bitcast.18, bf16[256,256]{1,0:T(8,128)(2,1)} %bitcast.19, ...), custom_call_target="tpu_custom_call" | custom-call | tf_op jit(solution)/shard_map/pallas_call | solution.py:613
  48.6 5.8 %shard_map.181 = (bf16[256,256]{1,0:T(8,128)(2,1)}, bf16[256,256]{1,0:T(8,128)(2,1)}, bf16[1024,1024]{1,0:T(8,128)(2,1)}, bf16[1024,128]{1,0:T(8,128)(2,1)}, bf1...) custom-call(bf16[2304,256]{1,0:T(8,128)(2,1)} %get-tuple-element.17.mn, ...), custom_call_target="tpu_custom_call" | custom-call | tf_op jit(solution)/shard_map/pallas_call | solution.py:694

commit v2 on v1

--- a/solution.py
+++ b/solution.py
@@ -19,6 +19,8 @@
 SCALE = 1.0 / math.sqrt(HD)
 LOG2E = math.log2(math.e)
 CHUNK = 512
+AHEAD = 3
+BEFORE = 4
 
 
 def rope_tables(length):
@@ -161,11 +163,9 @@
         pltpu.make_async_copy(stashed, cb.at[0], load_sem.at[steps, 3]),
     )
     small[0].start()
-    for i in range(steps):
+    for i in range(AHEAD):
         for copy in loads(i):
             copy.start()
-    for copy in small[1:]:
-        copy.start()
 
     gw_acc[...] = jnp.zeros_like(gw_acc)
     ws_acc[...] = jnp.zeros_like(ws_acc)
@@ -175,19 +175,22 @@
     def weight_step(i, _):
         rows = pl.ds(pl.multiple_of(i * CHUNK, CHUNK), CHUNK)
         copies = loads(i)
-        copies[0].wait()
+
+        @pl.when(i + AHEAD < steps)
+        def _():
+            for copy in loads(i + AHEAD):
+                copy.start()
+
+        for copy in copies:
+            copy.wait()
         s = s_v[rows, :]
         st = s.T
         st_v[:, rows] = st
         gram_acc[...] += nn(st, s)
         stg = (st.astype(F32) * gain_v[:, rows]).astype(BF16)
-        copies[1].wait()
         gw_acc[:, :eq] += nn(stg, wq_v[rows, :])
-        copies[2].wait()
         gw_acc[:, eq : eq + HD] += nn(stg, wk_v[rows, :])
-        copies[3].wait()
         gw_acc[:, eq + HD :] += nn(stg, wv_v[rows, :])
-        copies[4].wait()
         ws_acc[...] += nn(wo_v[:, rows], s)
         return 0
 
@@ -213,6 +216,9 @@
     sends = input_copies(sent_backward, sent_forward)
     edge_sends = input_copies(loss_grad, new_coeffs)
 
+    lax.fori_loop(0, BEFORE, weight_step, 0)
+    for copy in small[1:]:
+        copy.start()
     pl.semaphore_wait(barrier, len(others) + 3)
 
     @pl.when(p == 0)
@@ -243,7 +249,7 @@
 
     stash_across.start()
 
-    lax.fori_loop(0, steps, weight_step, 0)
+    lax.fori_loop(BEFORE, steps, weight_step, 0)
 
     gw_value = gw_acc[...].astype(BF16)
     gw[...] = gw_value
@@ -282,57 +288,72 @@
         values = (qkv[eq + HD :] * inverse).astype(BF16)
         return ct, ut, inverse, queries, keys, values
 
-    def softmax(keys_rows, query):
-        scores = jnp.where(causal, nn(keys_rows, query), -1e30)
-        powers = jnp.exp2(scores - jnp.max(scores, axis=0, keepdims=True))
-        return powers.astype(BF16), powers, 1.0 / jnp.sum(powers, axis=0, keepdims=True)
-
-    def backward(slot, initial, own):
-        c = cb[slot]
-        g = gb[slot]
-        ct, ut, inverse, queries, keys, values = project(c)
-        keys_rows = keys.T
-        values_rows = values.T
-        grads = nt(ws[...], g)
-        dk = jnp.zeros((HD, length), F32)
-        dv = jnp.zeros((HD, length), F32)
-        for i in range(heads):
-            rows = slice(i * HD, (i + 1) * HD)
-            low, powers, weight = softmax(keys_rows, queries[i])
-            out = nn(values, low) * weight
-            o_v[rows, :] = out.astype(BF16)
-            grad = (grads[rows] * weight).astype(BF16)
-            through = nn(values_rows, grad)
-            centre = jnp.sum(grad.astype(F32) * out, axis=0, keepdims=True)
-            ds = (powers * (through - centre)).astype(BF16)
-            dq = undo_rope(nn(keys, ds), cos, sin)
-            dt[rows, :] = (dq * (inverse * SCALE)).astype(BF16)
-            dk = dk + nt(queries[i], ds)
-            dv = dv + nt(grad, low)
-        dt[eq : eq + HD, :] = (undo_rope(dk, cos, sin) * (inverse * (1.0 / LOG2E))).astype(BF16)
-        dt[eq + HD :, :] = (dv * inverse).astype(BF16)
-        d = dt[...]
-        mt = nn(d, c)
-        nv = nn(o_v[...], g)
-        if initial:
-            mt_acc[...] = mt
-            n_acc[...] = nv
-        else:
-            mt_acc[...] += mt
-            n_acc[...] += nv
-        if not own:
-            return None
-        back = nn(gw[...], d)
-        middle = jnp.sum(back * ct.astype(F32), axis=0, keepdims=True)
-        return back - ut * (inverse * inverse * middle * (1.0 / width))
-
-    def forward(slot):
-        ct, ut, inverse, queries, keys, values = project(cf[slot])
-        keys_rows = keys.T
-        for i in range(heads):
-            low, _, weight = softmax(keys_rows, queries[i])
-            o_v[i * HD : (i + 1) * HD, :] = (nn(values, low) * weight).astype(BF16)
-        return ut, nn(wst[...], o_v[...])
+    def softmax(pairs):
+        scores = [jnp.where(causal, nn(keys_rows, query), -1e30) for keys_rows, query in pairs]
+        tops = [jnp.max(x, axis=0, keepdims=True) for x in scores]
+        powers = [jnp.exp2(x - top) for x, top in zip(scores, tops)]
+        weights = [1.0 / jnp.sum(x, axis=0, keepdims=True) for x in powers]
+        return [x.astype(BF16) for x in powers], powers, weights
+
+    def backward(slots, initial, own):
+        count = len(slots)
+        many = [(j, i) for j in range(count) for i in range(heads)]
+        cs = [cb[slot] for slot in slots]
+        gs = [gb[slot] for slot in slots]
+        projected = [project(c) for c in cs]
+        cts, uts, inverses, queries, keys, values = zip(*projected)
+        keys_rows = [x.T for x in keys]
+        values_rows = [x.T for x in values]
+        grads = [nt(ws[...], g) for g in gs]
+        low, powers, weights = softmax([(keys_rows[j], queries[j][i]) for j, i in many])
+        outs = [nn(values[j], x) * w for (j, _), x, w in zip(many, low, weights)]
+        grad = [
+            (grads[j][i * HD : (i + 1) * HD] * w).astype(BF16) for (j, i), w in zip(many, weights)
+        ]
+        through = [nn(values_rows[j], x) for (j, _), x in zip(many, grad)]
+        centre = [jnp.sum(x.astype(F32) * y, axis=0, keepdims=True) for x, y in zip(grad, outs)]
+        ds = [(x * (y - m)).astype(BF16) for x, y, m in zip(powers, through, centre)]
+        dq = [nn(keys[j], x) for (j, _), x in zip(many, ds)]
+        results = []
+        for j in range(count):
+            inverse = inverses[j]
+            dk = jnp.zeros((HD, length), F32)
+            dv = jnp.zeros((HD, length), F32)
+            for i in range(heads):
+                at = j * heads + i
+                rows = slice(i * HD, (i + 1) * HD)
+                o_v[j, rows, :] = outs[at].astype(BF16)
+                dt[j, rows, :] = (undo_rope(dq[at], cos, sin) * (inverse * SCALE)).astype(BF16)
+                dk = dk + nt(queries[j][i], ds[at])
+                dv = dv + nt(grad[at], low[at])
+            dt[j, eq : eq + HD, :] = (
+                undo_rope(dk, cos, sin) * (inverse * (1.0 / LOG2E))
+            ).astype(BF16)
+            dt[j, eq + HD :, :] = (dv * inverse).astype(BF16)
+            mt = nn(dt[j], cs[j])
+            nv = nn(o_v[j], gs[j])
+            if initial and j == 0:
+                mt_acc[...] = mt
+                n_acc[...] = nv
+            else:
+                mt_acc[...] += mt
+                n_acc[...] += nv
+            if own:
+                back = nn(gw[...], dt[j])
+                middle = jnp.sum(back * cts[j].astype(F32), axis=0, keepdims=True)
+                results.append(back - uts[j] * (inverse * inverse * middle * (1.0 / width)))
+        return results
+
+    def forward(slots):
+        count = len(slots)
+        many = [(j, i) for j in range(count) for i in range(heads)]
+        projected = [project(cf[slot]) for slot in slots]
+        _, uts, _, queries, keys, values = zip(*projected)
+        keys_rows = [x.T for x in keys]
+        low, _, weights = softmax([(keys_rows[j], queries[j][i]) for j, i in many])
+        for (j, i), x, w in zip(many, low, weights):
+            o_v[j, i * HD : (i + 1) * HD, :] = (nn(values[j], x) * w).astype(BF16)
+        return [(uts[j], nn(wst[...], o_v[j])) for j in range(count)]
 
     shard = rank // tensors
     mine = pl.ds(pl.multiple_of(z * shard, shard), shard)
@@ -401,39 +422,34 @@
 
     sends[0].wait_recv()
     relay_g0.start()
-    part[1] = backward(0, True, True)
-
     sends[1].wait_recv()
     relay_cf.start()
-    stash_pair.wait_recv()
-    relay_g0.wait_recv()
-    start_pair(1, backward(1, False, True))
-
-    ut, value = forward(0)
-    u_own[...] = ut[...]
-    part[0] = value
 
     sends[2].wait_recv()
     relay_g2.start()
     stash_across.wait_recv()
     relay_cb.start()
+    stash_pair.wait_recv()
+    relay_g0.wait_recv()
+    part[1], value = backward([0, 1], True, True)
+    start_pair(1, value)
+
+    relay_cf.wait_recv()
+    (first, second) = forward([0, 1])
+    u_own[...], part[0] = first
+    start_pair(0, second[1])
     start_scatter(1)
-    relay_cf.wait_recv()
-    _, value = forward(1)
-    start_pair(0, value)
+    relay_g2.wait_recv()
+    relay_cb.wait_recv()
+
+    start_scatter(0)
+    backward([2, 3], False, False)
 
     own_g = gb[0]
     lift = (
         nt(gram3[0, mine, :], own_g) + nt(gram3[1, mine, :], own_g) + nt(gram3[2, mine, :], own_g)
     )
     start_gather(1, lift)
-    backward(2, False, False)
-
-    start_scatter(0)
-    relay_g2.wait_recv()
-    relay_cb.wait_recv()
-    backward(3, False, False)
-
     start_gather(0, u_own[mine, :])
 
     m_value = mt_acc[...].astype(BF16)
@@ -490,7 +506,9 @@
         total = gg_recv[2 * hh] + gg_recv[2 * hh + 1]
         for zz in range(1, tensors):
             total = total + gg_recv[4 * zz + 2 * hh] + gg_recv[4 * zz + 2 * hh + 1]
-        gg_out[8 * hh : 8 * hh + 8, :] = total
+        for i in range(8):
+            at = hh * half_width + i * block
+            gg_out[:, at : at + block] = total[i : i + 1, :]
 
     for copy in exchange[1:]:
         copy.wait_recv()
@@ -526,9 +544,13 @@
     go_out,
     gain_out,
     mn_v,
+    fb_v,
+    fb_t,
     s_v,
     gain_v,
     gq_v,
+    gk_v,
+    gv_v,
     go_v,
     load_sem,
     out_sem,
@@ -536,24 +558,36 @@
     rows_own, eq, block = sizes
     n = lax.axis_index("dp")
     own = pl.ds(pl.multiple_of(n * rows_own, rows_own), rows_own)
+    n_at = eq + 2 * HD
     copies = (
         pltpu.make_async_copy(basis.at[own, :], s_v, load_sem.at[0]),
-        pltpu.make_async_copy(gain.at[:, own], gain_v, load_sem.at[1]),
-        pltpu.make_async_copy(mn, mn_v, load_sem.at[2]),
+        pltpu.make_async_copy(
+            mn.at[pl.ds(n_at, eq), :], mn_v.at[pl.ds(n_at, eq), :], load_sem.at[1]
+        ),
+        pltpu.make_async_copy(gain.at[:, own], gain_v, load_sem.at[2]),
+        pltpu.make_async_copy(mn.at[pl.ds(0, n_at), :], mn_v.at[pl.ds(0, n_at), :], load_sem.at[3]),
+        pltpu.make_async_copy(fb, fb_v, load_sem.at[4]),
     )
     for copy in copies:
         copy.start()
-    forward_out[...] = fb[0].T
-    backward_out[...] = fb[1].T
-    wide = gg.shape[1]
-    for i in range(gg.shape[0]):
-        gain_out[:, i * wide : (i + 1) * wide] = gg[i : i + 1, :]
-    for copy in copies:
+    outs = []
+
+    def send(src, dst):
+        copy = pltpu.make_async_copy(src, dst, out_sem.at[len(outs)])
+        copy.start()
+        outs.append(copy)
+
+    send(gg, gain_out)
+    for copy in copies[:2]:
+        copy.wait()
+    s = s_v[...]
+    for i in range(eq // block):
+        rows = slice(i * block, (i + 1) * block)
+        go_v[rows, :] = nt(mn_v[n_at + i * block : n_at + (i + 1) * block, :], s).astype(BF16)
+        send(go_v.at[rows, :], go_out.at[rows, :])
+    for copy in copies[2:]:
         copy.wait()
     gain_cols = jnp.broadcast_to(gain_v[...], (HD, rows_own)).T
-    n_at = eq + 2 * HD
-
-    outs = []
     for i in range(rows_own // block):
         rows = slice(i * block, (i + 1) * block)
         s = s_v[rows, :]
@@ -562,21 +596,16 @@
             cols = slice(2 * j * HD, 2 * (j + 1) * HD)
             value = nt(s, mn_v[cols, :])
             gq_v[rows, cols] = (value * jnp.concatenate([scale, scale], axis=1)).astype(BF16)
-        copy = pltpu.make_async_copy(gq_v.at[rows, :], gq_out.at[rows, :], out_sem.at[i])
-        copy.start()
-        outs.append(copy)
         value = nt(s, mn_v[eq:n_at, :])
-        gk_out[rows, :] = (value[:, :HD] * scale).astype(BF16)
-        gv_out[rows, :] = (value[:, HD:] * scale).astype(BF16)
-    s = s_v[...]
-    for i in range(eq // block):
-        rows = slice(i * block, (i + 1) * block)
-        go_v[rows, :] = nt(mn_v[n_at + i * block : n_at + (i + 1) * block, :], s).astype(BF16)
-        copy = pltpu.make_async_copy(
-            go_v.at[rows, :], go_out.at[rows, :], out_sem.at[rows_own // block + i]
-        )
-        copy.start()
-        outs.append(copy)
+        gk_v[rows, :] = (value[:, :HD] * scale).astype(BF16)
+        gv_v[rows, :] = (value[:, HD:] * scale).astype(BF16)
+        send(gq_v.at[rows, :], gq_out.at[rows, :])
+    send(gk_v, gk_out)
+    send(gv_v, gv_out)
+    fb_t[0] = fb_v[0].T
+    fb_t[1] = fb_v[1].T
+    send(fb_t.at[0], forward_out)
+    send(fb_t.at[1], backward_out)
     for copy in outs:
         copy.wait()
 
@@ -615,7 +644,7 @@
         out_shape=(
             jax.ShapeDtypeStruct((total, rank), BF16),
             jax.ShapeDtypeStruct((2, rank, length), BF16),
-            jax.ShapeDtypeStruct((16, width // 16), F32),
+            jax.ShapeDtypeStruct((1, width), F32),
         ),
         in_specs=[any_spec] * 13,
         out_specs=(any_spec, any_spec, vmem_spec),
@@ -642,8 +671,8 @@
             pltpu.VMEM((2, length, rank), BF16),
             pltpu.VMEM((eq + 2 * HD, rank), F32),
             pltpu.VMEM((eq, rank), F32),
-            pltpu.VMEM((eq + 2 * HD, length), BF16),
-            pltpu.VMEM((eq, length), BF16),
+            pltpu.VMEM((2, eq + 2 * HD, length), BF16),
+            pltpu.VMEM((2, eq, length), BF16),
             pltpu.VMEM((rank, length), F32),
             pltpu.VMEM((2, rank, length), F32),
             pltpu.VMEM((2, rank, length), BF16),
@@ -702,16 +731,20 @@
             jax.ShapeDtypeStruct((both, rows_own), BF16),
             jax.ShapeDtypeStruct((1, width), F32),
         ),
-        in_specs=[any_spec, vmem_spec, vmem_spec, any_spec, any_spec],
-        out_specs=(vmem_spec, vmem_spec, any_spec, vmem_spec, vmem_spec, any_spec, vmem_spec),
+        in_specs=[any_spec] * 5,
+        out_specs=(any_spec,) * 7,
         scratch_shapes=[
             pltpu.VMEM((total, rank), BF16),
+            pltpu.VMEM((2, rank, length), BF16),
+            pltpu.VMEM((2, length, rank), BF16),
             pltpu.VMEM((rows_own, rank), BF16),
             pltpu.VMEM((1, rows_own), F32),
             pltpu.VMEM((rows_own, both), BF16),
+            pltpu.VMEM((rows_own, HD), BF16),
+            pltpu.VMEM((rows_own, HD), BF16),
             pltpu.VMEM((both, rows_own), BF16),
-            dma((3,)),
-            dma((rows_own // block + both // block,)),
+            dma((5,)),
+            dma((rows_own // block + both // block + 5,)),
         ],
         compiler_params=pltpu.CompilerParams(vmem_limit_bytes=56 * 1024 * 1024),
     )(mn, fb, gg, subspace, norm_gain)

time: 54.8 us -> 43.7 us (0.80)
  Pallas kernels: 53.8 us -> 42.9 us
    pallas_call x1, Pallas kernels: 48 us -> 38.9 us  [body(): pl.pallas_call(functools.partial(main_kernel, (pipes, tensors, width, ran...]
    pallas_call x1, Pallas kernels: 5.77 us -> 4.03 us  [body(): pl.pallas_call(functools.partial(slice_kernel, (rows_own, both, block)),...]
where the time goes in v2:
time: 43.7 us; the launch traced here: 43.5 us
  Pallas kernels  42.9 us (98%)
  between operations  0.64 us (1%)
    pallas_call x1, Pallas kernels, body(): pl.pallas_call(functools.partial(main_kernel, (pipes, tensors, width, ran...  38.9 us
    pallas_call x1, Pallas kernels, body(): pl.pallas_call(functools.partial(slice_kernel, (rows_own, both, block)),...  4.03 us

profile of v2, /device:TPU:1, one launch (start us, length us, event | category | flops | bytes accessed | tf_op | source)
XLA Modules:
  0.0 43.5 jit_solution(11965211831378982106)
XLA Ops:
  0.6 38.9 %shard_map.180 = (bf16[2304,256]{1,0:T(8,128)(2,1)}, bf16[2,256,256]{2,1,0:T(8,128)(2,1)}, f32[1,4096]{1,0:T(1,128)}) custom-call(bf16[256,256]{1,0:T(8,128)(2,1)} %new_coeffs.1, bf16[256,256]{1,0:T(8,128)(2,1)} %loss_grad.1, bf16[256,256]{1,0:T(8,128)(2,1)} %bitcast.17, bf16[256,256]{1,0:T(8,128)(2,1)} %bitcast.18, bf16[256,256]{1,0:T(8,128)(2,1)} %bitcast.19, ...), custom_call_target="tpu_custom_call" | custom-call | tf_op jit(solution)/shard_map/pallas_call | solution.py:642
  39.5 4.0 %shard_map.181 = (bf16[256,256]{1,0:T(8,128)(2,1)}, bf16[256,256]{1,0:T(8,128)(2,1)}, bf16[1024,1024]{1,0:T(8,128)(2,1)}, bf16[1024,128]{1,0:T(8,128)(2,1)}, bf1...) custom-call(bf16[2304,256]{1,0:T(8,128)(2,1)} %get-tuple-element.17.mn, ...), custom_call_target="tpu_custom_call" | custom-call | tf_op jit(solution)/shard_map/pallas_call | solution.py:723

commit v3 on v2

--- a/solution.py
+++ b/solution.py
@@ -20,7 +20,8 @@
 LOG2E = math.log2(math.e)
 CHUNK = 512
 AHEAD = 3
-BEFORE = 4
+BEFORE = 1
+LATER = 3
 
 
 def rope_tables(length):
@@ -71,9 +72,7 @@
     gain_v,
     cos_v,
     sin_v,
-    wq_v,
-    wk_v,
-    wv_v,
+    w_v,
     wo_v,
     gw_acc,
     ws_acc,
@@ -90,6 +89,7 @@
     n_acc,
     dt,
     o_v,
+    o_f,
     u_own,
     part,
     pair_send,
@@ -97,11 +97,15 @@
     rs_send,
     rs_recv,
     shard_v,
+    lift_v,
     m_v,
     n_v,
     kv_recv,
     gg_part,
+    gg_pair_recv,
+    gg_half,
     gg_recv,
+    gg_total,
     load_sem,
     in_sem,
     in_send,
@@ -128,10 +132,12 @@
     across = 2 * (1 - h) + k
     after = lax.rem(p + 1, pipes)
     before = lax.rem(p + pipes - 1, pipes)
-    others = [(dz, dn) for dz in range(tensors) for dn in range(4) if (dz, dn) != (0, 0)]
     others = [
-        (lax.rem(z + dz, tensors), lax.rem(n + dn, 4)) for dz, dn in others
-    ]
+        (lax.rem(z + dz, tensors), lax.rem(n + 2 * dh, 4))
+        for dz in range(tensors)
+        for dh in range(2)
+        if (dz, dh) != (0, 0)
+    ] + [(z, partner)]
 
     barrier = pltpu.get_barrier_semaphore()
     for oz, on in others:
@@ -147,10 +153,14 @@
         return (
             pltpu.make_async_copy(basis.at[rows, :], s_v.at[rows, :], load_sem.at[i, 0]),
             pltpu.make_async_copy(
-                w_query.at[rows, pl.ds(col, eq)], wq_v.at[rows, :], load_sem.at[i, 1]
+                w_query.at[rows, pl.ds(col, eq)], w_v.at[rows, pl.ds(0, eq)], load_sem.at[i, 1]
             ),
-            pltpu.make_async_copy(w_key.at[rows, :], wk_v.at[rows, :], load_sem.at[i, 2]),
-            pltpu.make_async_copy(w_value.at[rows, :], wv_v.at[rows, :], load_sem.at[i, 3]),
+            pltpu.make_async_copy(
+                w_key.at[rows, :], w_v.at[rows, pl.ds(eq, HD)], load_sem.at[i, 2]
+            ),
+            pltpu.make_async_copy(
+                w_value.at[rows, :], w_v.at[rows, pl.ds(eq + HD, HD)], load_sem.at[i, 3]
+            ),
             pltpu.make_async_copy(
                 w_output.at[pl.ds(col, eq), rows], wo_v.at[:, rows], load_sem.at[i, 4]
             ),
@@ -188,9 +198,7 @@
         st_v[:, rows] = st
         gram_acc[...] += nn(st, s)
         stg = (st.astype(F32) * gain_v[:, rows]).astype(BF16)
-        gw_acc[:, :eq] += nn(stg, wq_v[rows, :])
-        gw_acc[:, eq : eq + HD] += nn(stg, wk_v[rows, :])
-        gw_acc[:, eq + HD :] += nn(stg, wv_v[rows, :])
+        gw_acc[...] += nn(stg, w_v[rows, :])
         ws_acc[...] += nn(wo_v[:, rows], s)
         return 0
 
@@ -221,35 +229,22 @@
         copy.start()
     pl.semaphore_wait(barrier, len(others) + 3)
 
-    @pl.when(p == 0)
-    def _():
-        edge_sends[0].start()
-
-    @pl.when(p != 0)
-    def _():
-        sends[0].start()
-
+    def send_input(i, edge):
+        @pl.when(p == edge)
+        def _():
+            edge_sends[i].start()
+
+        @pl.when(p != edge)
+        def _():
+            sends[i].start()
+
+    send_input(1, pipes - 1)
     stash_pair.start()
-
-    @pl.when(p == pipes - 1)
-    def _():
-        edge_sends[1].start()
-
-    @pl.when(p != pipes - 1)
-    def _():
-        sends[1].start()
-
-    @pl.when(p == 0)
-    def _():
-        edge_sends[2].start()
-
-    @pl.when(p != 0)
-    def _():
-        sends[2].start()
-
+    lax.fori_loop(BEFORE, LATER, weight_step, 0)
+    send_input(0, 0)
+    send_input(2, 0)
     stash_across.start()
-
-    lax.fori_loop(BEFORE, steps, weight_step, 0)
+    lax.fori_loop(LATER, steps, weight_step, 0)
 
     gw_value = gw_acc[...].astype(BF16)
     gw[...] = gw_value
@@ -295,18 +290,21 @@
         weights = [1.0 / jnp.sum(x, axis=0, keepdims=True) for x in powers]
         return [x.astype(BF16) for x in powers], powers, weights
 
-    def backward(slots, initial, own):
+    def backward(slots, initial, own, between, later):
         count = len(slots)
         many = [(j, i) for j in range(count) for i in range(heads)]
         cs = [cb[slot] for slot in slots]
-        gs = [gb[slot] for slot in slots]
         projected = [project(c) for c in cs]
         cts, uts, inverses, queries, keys, values = zip(*projected)
         keys_rows = [x.T for x in keys]
         values_rows = [x.T for x in values]
-        grads = [nt(ws[...], g) for g in gs]
         low, powers, weights = softmax([(keys_rows[j], queries[j][i]) for j, i in many])
         outs = [nn(values[j], x) * w for (j, _), x, w in zip(many, low, weights)]
+        for at, (j, i) in enumerate(many):
+            o_v[j, i * HD : (i + 1) * HD, :] = outs[at].astype(BF16)
+        between()
+        gs = [gb[slot] for slot in slots]
+        grads = [nt(ws[...], g) for g in gs]
         grad = [
             (grads[j][i * HD : (i + 1) * HD] * w).astype(BF16) for (j, i), w in zip(many, weights)
         ]
@@ -314,6 +312,16 @@
         centre = [jnp.sum(x.astype(F32) * y, axis=0, keepdims=True) for x, y in zip(grad, outs)]
         ds = [(x * (y - m)).astype(BF16) for x, y, m in zip(powers, through, centre)]
         dq = [nn(keys[j], x) for (j, _), x in zip(many, ds)]
+        for at, (j, i) in enumerate(many):
+            value = undo_rope(dq[at], cos, sin) * (inverses[j] * SCALE)
+            dt[j, i * HD : (i + 1) * HD, :] = value.astype(BF16)
+        for j in range(count):
+            nv = nn(o_v[j], gs[j])
+            if initial and j == 0:
+                n_acc[...] = nv
+            else:
+                n_acc[...] += nv
+        later()
         results = []
         for j in range(count):
             inverse = inverses[j]
@@ -321,9 +329,6 @@
             dv = jnp.zeros((HD, length), F32)
             for i in range(heads):
                 at = j * heads + i
-                rows = slice(i * HD, (i + 1) * HD)
-                o_v[j, rows, :] = outs[at].astype(BF16)
-                dt[j, rows, :] = (undo_rope(dq[at], cos, sin) * (inverse * SCALE)).astype(BF16)
                 dk = dk + nt(queries[j][i], ds[at])
                 dv = dv + nt(grad[at], low[at])
             dt[j, eq : eq + HD, :] = (
@@ -331,13 +336,10 @@
             ).astype(BF16)
             dt[j, eq + HD :, :] = (dv * inverse).astype(BF16)
             mt = nn(dt[j], cs[j])
-            nv = nn(o_v[j], gs[j])
             if initial and j == 0:
                 mt_acc[...] = mt
-                n_acc[...] = nv
             else:
                 mt_acc[...] += mt
-                n_acc[...] += nv
             if own:
                 back = nn(gw[...], dt[j])
                 middle = jnp.sum(back * cts[j].astype(F32), axis=0, keepdims=True)
@@ -352,8 +354,8 @@
         keys_rows = [x.T for x in keys]
         low, _, weights = softmax([(keys_rows[j], queries[j][i]) for j, i in many])
         for (j, i), x, w in zip(many, low, weights):
-            o_v[j, i * HD : (i + 1) * HD, :] = (nn(values[j], x) * w).astype(BF16)
-        return [(uts[j], nn(wst[...], o_v[j])) for j in range(count)]
+            o_f[j, i * HD : (i + 1) * HD, :] = (nn(values[j], x) * w).astype(BF16)
+        return [(uts[j], nn(wst[...], o_f[j])) for j in range(count)]
 
     shard = rank // tensors
     mine = pl.ds(pl.multiple_of(z * shard, shard), shard)
@@ -420,103 +422,132 @@
     relay_g2 = remote(gb.at[2], gb.at[3], relay_send.at[2], in_sem.at[7], (p, z, partner))
     relay_cb = remote(cb.at[2], cb.at[3], relay_send.at[3], in_sem.at[8], (p, z, partner))
 
-    sends[0].wait_recv()
-    relay_g0.start()
+    q_rows = pl.ds(pl.multiple_of(k * eq, eq), eq)
+    kv_rows = pl.ds(2 * eq, 2 * HD)
+    n_rows = pl.ds(pl.multiple_of(2 * eq + 2 * HD + k * eq, HD), eq)
+    own_m = m_v.at[pl.ds(0, eq), :]
+    own_kv = m_v.at[pl.ds(eq, 2 * HD), :]
+    peer = (p, z, partner)
+    exchange = (
+        remote(n_v, mn_out.at[n_rows, :], m_ssem.at[0], m_rsem.at[0], peer),
+        remote(mt_acc.at[pl.ds(eq, 2 * HD), :], kv_recv, m_ssem.at[1], m_rsem.at[1], peer),
+        remote(own_m, mn_out.at[q_rows, :], m_ssem.at[2], m_rsem.at[2], peer),
+    )
+    keep = (
+        pltpu.make_async_copy(n_v, mn_out.at[n_rows, :], own_sem.at[2]),
+        pltpu.make_async_copy(own_m, mn_out.at[q_rows, :], own_sem.at[3]),
+        pltpu.make_async_copy(own_kv, mn_out.at[kv_rows, :], own_sem.at[4]),
+    )
+
+    chips = [(dz, dh) for dz in range(tensors) for dh in range(2) if (dz, dh) != (0, 0)]
+    gg_pair = remote(
+        gg_part.at[1 - k], gg_pair_recv, gg_ssem.at[0], gg_rsem.at[0], (p, z, partner)
+    )
+    gg_last = remote(gg_total.at[k], gg_total.at[k], gg_ssem.at[1], gg_rsem.at[1], (p, z, partner))
+    gg_copies = [
+        remote(
+            gg_half,
+            gg_recv.at[i],
+            gg_ssem.at[i + 2],
+            gg_rsem.at[i + 2],
+            (p, lax.rem(z + dz, tensors), lax.rem(n + 2 * dh, 4)),
+        )
+        for i, (dz, dh) in enumerate(chips)
+    ]
+
+    def gain_stage():
+        gg_pair.wait_recv()
+        gg_half[...] = gg_part[k] + gg_pair_recv[...]
+        for copy in gg_copies:
+            copy.start()
+
+    def gain_finish():
+        total = gg_half[...]
+        for copy in gg_copies:
+            copy.wait_recv()
+        for i in range(len(gg_copies)):
+            total = total + gg_recv[i]
+        gg_total[k] = total
+        gg_last.start()
+
+    block = width // 8
+    fine = width // 16
+
+    def gain_terms():
+        terms = mt_acc[...].astype(BF16)
+        for i in range(8):
+            rows = slice(i * block, (i + 1) * block)
+            lifted = nn(w_v[rows, :], terms)
+            product = lifted * s_v[rows, :].astype(F32)
+            product = sum(product[:, j : j + HD] for j in range(HD, rank, HD)) + product[:, :HD]
+            row = jnp.sum(product.T, axis=0, keepdims=True)
+            at = 2 * (i % 4)
+            gg_part[i // 4, at : at + 1, :] = row[:, :fine]
+            gg_part[i // 4, at + 1 : at + 2, :] = row[:, fine:]
+        gg_pair.start()
+
+    def between_own():
+        sends[0].wait_recv()
+        relay_g0.start()
+        relay_cf.wait_recv()
+        first, second = forward([0, 1])
+        u_own[...], part[0] = first
+        start_pair(0, second[1])
+        relay_g0.wait_recv()
+
+    def between_across():
+        relay_g2.wait_recv()
+        gain_stage()
+        own_g = gb[0]
+        lift_v[...] = (
+            nt(gram3[0, mine, :], own_g)
+            + nt(gram3[1, mine, :], own_g)
+            + nt(gram3[2, mine, :], own_g)
+        )
+
+    def later_across():
+        n_v[...] = n_acc[...].astype(BF16)
+        exchange[0].start()
+        keep[0].start()
+        start_gather(0, u_own[mine, :])
+
     sends[1].wait_recv()
     relay_cf.start()
-
+    stash_pair.wait_recv()
+    part[1], value = backward([0, 1], True, True, between_own, lambda: None)
+    start_pair(1, value)
+    start_scatter(0)
     sends[2].wait_recv()
     relay_g2.start()
     stash_across.wait_recv()
     relay_cb.start()
-    stash_pair.wait_recv()
-    relay_g0.wait_recv()
-    part[1], value = backward([0, 1], True, True)
-    start_pair(1, value)
-
-    relay_cf.wait_recv()
-    (first, second) = forward([0, 1])
-    u_own[...], part[0] = first
-    start_pair(0, second[1])
+    gain_terms()
     start_scatter(1)
-    relay_g2.wait_recv()
     relay_cb.wait_recv()
-
-    start_scatter(0)
-    backward([2, 3], False, False)
-
-    own_g = gb[0]
-    lift = (
-        nt(gram3[0, mine, :], own_g) + nt(gram3[1, mine, :], own_g) + nt(gram3[2, mine, :], own_g)
-    )
-    start_gather(1, lift)
-    start_gather(0, u_own[mine, :])
-
-    m_value = mt_acc[...].astype(BF16)
-    m_v[...] = m_value
-    n_v[...] = n_acc[...].astype(BF16)
-    kv_rows = pl.ds(2 * eq, 2 * HD)
-    q_rows = pl.ds(pl.multiple_of(k * eq, eq), eq)
-    n_rows = pl.ds(pl.multiple_of(2 * eq + 2 * HD + k * eq, HD), eq)
-    peer = (p, z, partner)
-    exchange = (
-        remote(mt_acc.at[pl.ds(eq, 2 * HD), :], kv_recv, m_ssem.at[0], m_rsem.at[0], peer),
-        remote(m_v.at[pl.ds(0, eq), :], mn_out.at[q_rows, :], m_ssem.at[1], m_rsem.at[1], peer),
-        remote(n_v, mn_out.at[n_rows, :], m_ssem.at[2], m_rsem.at[2], peer),
-    )
-    keep = (
-        pltpu.make_async_copy(m_v.at[pl.ds(0, eq), :], mn_out.at[q_rows, :], own_sem.at[2]),
-        pltpu.make_async_copy(n_v, mn_out.at[n_rows, :], own_sem.at[3]),
-    )
-    for copy in exchange + keep:
-        copy.start()
-
-    m_nat = m_value.T
-    half_width = width // 2
-    block = half_width // 8
-    for i in range(8):
-        rows = pl.ds(pl.multiple_of(h * half_width + i * block, block), block)
-        lifted = (
-            nt(m_nat[:, :eq], wq_v[rows, :])
-            + nt(m_nat[:, eq : eq + HD], wk_v[rows, :])
-            + nt(m_nat[:, eq + HD :], wv_v[rows, :])
-        )
-        gg_part[i : i + 1, :] = jnp.sum(lifted * st_v[:, rows].astype(F32), axis=0, keepdims=True)
-    me = z * 4 + n
-    gg_copies = [
-        remote(gg_part, gg_recv.at[me], gg_ssem.at[i], gg_rsem.at[me], (p, oz, on))
-        for i, (oz, on) in enumerate(others)
-    ]
-    for copy in gg_copies:
-        copy.start()
+    backward([2, 3], False, False, between_across, later_across)
+
+    exchange[1].start()
+    m_v[:eq, :] = mt_acc[:eq, :].astype(BF16)
+    exchange[2].start()
+    keep[1].start()
+    start_gather(1, lift_v[...])
+    gain_finish()
+    exchange[1].wait_recv()
+    m_v[eq:, :] = (mt_acc[eq:, :] + kv_recv[...]).astype(BF16)
+    keep[2].start()
+    gg_last.wait_recv()
+    for i in range(2):
+        for j in range(8):
+            at = (i * 8 + j) * fine
+            gg_out[:, at : at + fine] = gg_total[i, j : j + 1, :]
 
     exchange[0].wait_recv()
-    kv_total = mt_acc[eq:, :] + kv_recv[...]
-    m_v[eq:, :] = kv_total.astype(BF16)
-    kv_keep = pltpu.make_async_copy(
-        m_v.at[pl.ds(eq, 2 * HD), :], mn_out.at[kv_rows, :], own_sem.at[4]
-    )
-    kv_keep.start()
-
-    gg_recv[me] = gg_part[...]
-    for oz, on in others:
-        it = oz * 4 + on
-        remote(gg_part, gg_recv.at[it], gg_ssem.at[0], gg_rsem.at[it], (p, oz, on)).wait_recv()
-    for hh in range(2):
-        total = gg_recv[2 * hh] + gg_recv[2 * hh + 1]
-        for zz in range(1, tensors):
-            total = total + gg_recv[4 * zz + 2 * hh] + gg_recv[4 * zz + 2 * hh + 1]
-        for i in range(8):
-            at = hh * half_width + i * block
-            gg_out[:, at : at + block] = total[i : i + 1, :]
-
-    for copy in exchange[1:]:
-        copy.wait_recv()
+    exchange[2].wait_recv()
     for copy in exchange:
         copy.wait_send()
-    for copy in keep + (kv_keep,):
+    for copy in keep:
         copy.wait()
-    for copy in gg_copies:
+    for copy in gg_copies + [gg_pair, gg_last]:
         copy.wait_send()
     for i in range(2):
         own_copy(i).wait()
@@ -654,9 +685,7 @@
             pltpu.VMEM((1, width), F32),
             pltpu.VMEM((HALF, length), F32),
             pltpu.VMEM((HALF, length), F32),
-            pltpu.VMEM((width, eq), BF16),
-            pltpu.VMEM((width, HD), BF16),
-            pltpu.VMEM((width, HD), BF16),
+            pltpu.VMEM((width, eq + 2 * HD), BF16),
             pltpu.VMEM((eq, width), BF16),
             pltpu.VMEM((rank, eq + 2 * HD), F32),
             pltpu.VMEM((eq, rank), F32),
@@ -673,6 +702,7 @@
             pltpu.VMEM((eq, rank), F32),
             pltpu.VMEM((2, eq + 2 * HD, length), BF16),
             pltpu.VMEM((2, eq, length), BF16),
+            pltpu.VMEM((2, eq, length), BF16),
             pltpu.VMEM((rank, length), F32),
             pltpu.VMEM((2, rank, length), F32),
             pltpu.VMEM((2, rank, length), BF16),
@@ -680,11 +710,15 @@
             pltpu.VMEM((2, rank, length), BF16),
             pltpu.VMEM((2, tensors, shard, length), BF16),
             pltpu.VMEM((2, shard, length), BF16),
+            pltpu.VMEM((shard, length), F32),
             pltpu.VMEM((eq + 2 * HD, rank), BF16),
             pltpu.VMEM((eq, rank), BF16),
             pltpu.VMEM((2 * HD, rank), F32),
+            pltpu.VMEM((2, 8, width // 16), F32),
             pltpu.VMEM((8, width // 16), F32),
-            pltpu.VMEM((4 * tensors, 8, width // 16), F32),
+            pltpu.VMEM((8, width // 16), F32),
+            pltpu.VMEM((2 * tensors, 8, width // 16), F32),
+            pltpu.VMEM((2, 8, width // 16), F32),
             dma((steps + 1, 5)),
             dma((9,)),
             dma((5,)),
@@ -697,8 +731,8 @@
             dma((5,)),
             dma((3,)),
             dma((3,)),
-            dma((4 * tensors,)),
-            dma((4 * tensors,)),
+            dma((2 * tensors + 1,)),
+            dma((2 * tensors + 1,)),
         ],
         compiler_params=pltpu.CompilerParams(
             collective_id=0, has_side_effects=True, vmem_limit_bytes=56 * 1024 * 1024

time: 43.7 us -> 38.7 us (0.89)
  the two profiles are of different devices: /device:TPU:1 before, /device:TPU:8 now
where the time goes in v3:
time: 38.7 us; the launch traced here: 38.5 us
  Pallas kernels  37.9 us (98%)
  between operations  0.64 us (2%)
    pallas_call x1, Pallas kernels, body(): pl.pallas_call(functools.partial(main_kernel, (pipes, tensors, width, ran...  33.8 us
    pallas_call x1, Pallas kernels, body(): pl.pallas_call(functools.partial(slice_kernel, (rows_own, both, block)),...  4.03 us

profile of v3, /device:TPU:8, one launch (start us, length us, event | category | flops | bytes accessed | tf_op | source)
XLA Modules:
  0.0 38.5 jit_solution(6642496399476477788)
XLA Ops:
  0.6 33.8 %shard_map.180 = (bf16[2304,256]{1,0:T(8,128)(2,1)}, bf16[2,256,256]{2,1,0:T(8,128)(2,1)}, f32[1,4096]{1,0:T(1,128)}) custom-call(bf16[256,256]{1,0:T(8,128)(2,1)} %new_coeffs.1, bf16[256,256]{1,0:T(8,128)(2,1)} %loss_grad.1, bf16[256,256]{1,0:T(8,128)(2,1)} %bitcast.17, bf16[256,256]{1,0:T(8,128)(2,1)} %bitcast.18, bf16[256,256]{1,0:T(8,128)(2,1)} %bitcast.19, ...), custom_call_target="tpu_custom_call" | custom-call | tf_op jit(solution)/shard_map/pallas_call | solution.py:673
  34.5 4.0 %shard_map.181 = (bf16[256,256]{1,0:T(8,128)(2,1)}, bf16[256,256]{1,0:T(8,128)(2,1)}, bf16[1024,1024]{1,0:T(8,128)(2,1)}, bf16[1024,128]{1,0:T(8,128)(2,1)}, bf1...) custom-call(bf16[2304,256]{1,0:T(8,128)(2,1)} %get-tuple-element.17.mn, ...), custom_call_target="tpu_custom_call" | custom-call | tf_op jit(solution)/shard_map/pallas_call | solution.py:757
